TPU v7x, 512 devices: a whole 4x4x16 slice. The times are simulated.
512 devices in a mesh: case: 8 (over x, core), slab: 64 (over y, z).
Axes of the slice: x: 4, y: 4, z: 16, core: 2. Of those that a mesh axis runs over, the one named last changes fastest.
Arguments:
- sensitivity: float32 [8, 8388608], P('case', 'slab'), may hold values from -300 to 300
- material_share_now: float32 [64, 8, 16384], P('slab', 'case'), may hold values from 0.05 to 0.95
- material_share_prior: float32 [64, 8, 16384], P('slab', 'case'), may hold values from 0.05 to 0.95
- material_share_prior_prior: float32 [64, 8, 16384], P('slab', 'case'), may hold values from 0.05 to 0.95
- floor_asym_gap: float32 [64, 8, 16384], P('slab', 'case'), may hold values from 0.005 to 0.5
- ceiling_asym_gap: float32 [64, 8, 16384], P('slab', 'case'), may hold values from 0.005 to 0.5
- volume_weight: float32 [64, 8, 16384], P('slab', 'case'), may hold values from 0.5 to 2
- case_values: float32 [8], replicated, may hold values from 0.5 to 1.5
- duals_start: float32 [9], replicated, may hold values from 0.05 to 0.5
Outputs:
- new_design: float32 [64, 8, 16384], P('slab', 'case')
- lower_asym: float32 [64, 8, 16384], P('slab', 'case')
- upper_asym: float32 [64, 8, 16384], P('slab', 'case')
- duals: float32 [9], replicated
All inputs are finite; a program needn't handle non-finite values.
Results may differ from a plain program's by a relative error of at most 0.0003.
Values sent between devices are 32-bit elements; how exact they have to be, the bound alone decides.
No kernel may reach another device: no remote copies, remote signals or barrier semaphores. Data moves between devices by JAX's collectives and lax.ppermute only.
A program may use at most 64 MiB of HBM per device.

v0:
```python
import jax
import jax.numpy as jnp
from jax import lax
from jax.sharding import PartitionSpec as P

NEWTON = 4


PROX = 0.1
VOLFRAC = 0.4


def limit_couple(
    material_share_now,
    material_share_prior,
    material_share_prior_prior,
    floor_asym_gap,
    ceiling_asym_gap,
):
    trend = (material_share_now - material_share_prior) * (
        material_share_prior - material_share_prior_prior
    )
    factor = jnp.where(trend > 0, 1.2, jnp.where(trend < 0, 0.7, 1.0)).astype(
        material_share_now.dtype
    )
    minimal_limit = jnp.minimum(
        material_share_now - factor * floor_asym_gap, material_share_now - 0.01
    )
    maximal_limit = jnp.maximum(
        material_share_now + factor * ceiling_asym_gap, material_share_now + 0.01
    )
    return (minimal_limit, maximal_limit)


def bounds(material_share_now, minimal_limit, maximal_limit):
    floor_x = jnp.maximum(
        jnp.maximum(
            minimal_limit + 0.1 * (material_share_now - minimal_limit), material_share_now - 0.2
        ),
        0.0,
    )
    ceil_x = jnp.minimum(
        jnp.minimum(
            maximal_limit - 0.1 * (maximal_limit - material_share_now), material_share_now + 0.2
        ),
        1.0,
    )
    above = (maximal_limit - material_share_now) ** 2
    below = (material_share_now - minimal_limit) ** 2
    return (floor_x, ceil_x, above, below)


def weighted(material_share_now, minimal_limit, maximal_limit, above, below, slopes):
    rising = jnp.maximum(slopes, 0.0)
    falling = jnp.maximum(-slopes, 0.0)
    upward = above * (1.001 * rising + 0.001 * falling)
    downward = below * (0.001 * rising + 1.001 * falling)
    at_start = upward / (maximal_limit - material_share_now) + downward / (
        material_share_now - minimal_limit
    )
    return (upward, downward, at_start)


def place(big_p, big_q, minimal_limit, maximal_limit, floor_x, ceil_x):
    root_p = jnp.sqrt(big_p)
    root_q = jnp.sqrt(big_q)
    free_x = (root_p * minimal_limit + root_q * maximal_limit) / (root_p + root_q)
    chosen = jnp.minimum(jnp.maximum(free_x, floor_x), ceil_x)
    inside = jnp.where((free_x > floor_x) & (free_x < ceil_x), 1.0, 0.0).astype(free_x.dtype)
    return (chosen, inside)


def measure(upward, downward, chosen, inside, big_p, big_q, minimal_limit, maximal_limit):
    to_upper = maximal_limit - chosen
    to_lower = chosen - minimal_limit
    values = upward / to_upper + downward / to_lower
    slope = upward / (to_upper * to_upper) - downward / (to_lower * to_lower)
    curve = 2.0 * big_p / to_upper**3 + 2.0 * big_q / to_lower**3
    scaled = slope * jnp.sqrt(inside / curve)
    return (values, scaled)


def solve_small(matrix, vector):
    dual_count = vector.shape[0]
    factor_l = jnp.linalg.cholesky(matrix)
    forward = []
    for row_at in range(dual_count):
        running = vector[row_at]
        for col_at in range(row_at):
            running = running - factor_l[row_at, col_at] * forward[col_at]
        forward.append(running / factor_l[row_at, row_at])
    backward = [None] * dual_count
    for row_at in reversed(range(dual_count)):
        running = forward[row_at]
        for col_at in range(row_at + 1, dual_count):
            running = running - factor_l[col_at, row_at] * backward[col_at]
        backward[row_at] = running / factor_l[row_at, row_at]
    return jnp.stack(backward)


def advance(duals, grad_total, hess_total, case_values, element_total):
    dual_count = duals.shape[0]
    coupling = jnp.concatenate(
        [jnp.ones((dual_count - 1,), duals.dtype), jnp.zeros((1,), duals.dtype)]
    )
    excess = jnp.sum(duals[:-1]) - 1.0
    height = jnp.maximum(excess, 0.0)
    active = jnp.where(excess > 0, 1.0, 0.0).astype(duals.dtype)
    target = jnp.concatenate([case_values, jnp.full((1,), -VOLFRAC, duals.dtype)])
    gradient = grad_total / element_total + target - coupling * height
    negative = hess_total / element_total + coupling[:, None] * coupling[None, :] * active
    damping = 0.5 * jnp.trace(negative) / dual_count + 0.0001
    matrix = negative + damping * jnp.eye(dual_count, dtype=duals.dtype)
    step_dual = solve_small(matrix, gradient)
    return jnp.maximum(duals + step_dual, 0.1 * duals)


def per_device(
    sensitivity,
    material_share_now,
    material_share_prior,
    material_share_prior_prior,
    floor_asym_gap,
    ceiling_asym_gap,
    volume_weight,
    case_values,
    duals_start,
):
    case_count = lax.axis_size("case")
    slab_count = lax.axis_size("slab")
    owned = sensitivity.shape[0]
    slab_width = sensitivity.shape[1]
    piece = slab_width // case_count
    all_cases = owned * case_count
    element_total = jnp.asarray(piece * case_count * slab_count, jnp.float32)
    local_design = material_share_now.reshape(-1)
    local_weight = volume_weight.reshape(-1)
    minimal_limit, maximal_limit = limit_couple(
        local_design,
        material_share_prior.reshape(-1),
        material_share_prior_prior.reshape(-1),
        floor_asym_gap.reshape(-1),
        ceiling_asym_gap.reshape(-1),
    )
    regrouped = lax.all_to_all(
        sensitivity.reshape(owned, case_count, piece),
        "case",
        split_axis=1,
        concat_axis=0,
        tiled=True,
    )
    slopes = jnp.concatenate([regrouped.reshape(all_cases, piece), local_weight[None]], 0)
    floor_x, ceil_x, above, below = bounds(local_design, minimal_limit, maximal_limit)
    upward, downward, at_start = weighted(
        local_design, minimal_limit, maximal_limit, above, below, slopes
    )
    offset_local = -jnp.sum(at_start, 1) + jnp.concatenate(
        [jnp.zeros((all_cases,), jnp.float32), jnp.sum(local_weight * local_design)[None]]
    )

    def evaluate(duals, final):
        big_p = PROX * above + jnp.dot(duals, upward, precision=lax.Precision.HIGHEST)
        big_q = PROX * below + jnp.dot(duals, downward, precision=lax.Precision.HIGHEST)
        chosen, inside = place(big_p, big_q, minimal_limit, maximal_limit, floor_x, ceil_x)
        if final:
            return chosen
        values, scaled = measure(
            upward, downward, chosen, inside, big_p, big_q, minimal_limit, maximal_limit
        )
        hessian = jnp.dot(scaled, scaled.T, precision=lax.Precision.HIGHEST)
        return (jnp.sum(values, 1), hessian)

    offset_total = lax.psum(offset_local, ("case", "slab"))
    duals = duals_start
    for newton_step in range(NEWTON):
        grad_local, hess_local = evaluate(duals, False)
        grad_total, hess_total = lax.psum((grad_local, hess_local), ("case", "slab"))
        grad_total = grad_total + offset_total
        duals = advance(duals, grad_total, hess_total, case_values, element_total)
    chosen = evaluate(duals, True)
    return (
        chosen.reshape(1, 1, piece),
        minimal_limit.reshape(1, 1, piece),
        maximal_limit.reshape(1, 1, piece),
        duals,
    )


def solution(mesh):
    in_specs = (
        P("case", "slab"),
        P("slab", "case", None),
        P("slab", "case", None),
        P("slab", "case", None),
        P("slab", "case", None),
        P("slab", "case", None),
        P("slab", "case", None),
        P(),
        P(),
    )
    out_specs = (P("slab", "case", None), P("slab", "case", None), P("slab", "case", None), P())
    return jax.shard_map(
        per_device, mesh=mesh, in_specs=in_specs, out_specs=out_specs, check_vma=False
    )
```

profile of v0, /device:TPU:1, one launch (start us, length us, event | category | flops | bytes accessed | tf_op | source)
XLA Modules:
  0.0 728.7 jit_solution(8614338762495679185)
XLA Ops:
  0.7 10.4 %all-to-all-start = ((f32[1,8,16384]{2,0,1:T(1,128)}), f32[1,8,16384]{2,0,1:T(1,128)S(1)}, u32[]{:S(2)}, u32[]{:S(2)}) async-start(f32[1,8,16384]{2,0,1:T(1,128)} %bitcast.360), calls=%async_computation | async-start | bytes 1048576 | tf_op jit(solution)/shard_map/all_to_all | solution.py:145
  11.1 0.9 add_maximum_fusion
  12.0 0.7 add_minimum_fusion
  14.7 5.9 all-to-all-done
  20.9 1.1 fusion.61
  22.0 1.1 fusion.63
  23.4 1.1 add_reduce_fusion.3
  24.4 0.7 pad_add_fusion
  25.2 1.8 fusion.18
  27.0 104.5 %all-reduce.4 = (f32[9]{0:T(128)S(1)}, f32[9]{0:T(128)S(1)}, f32[9,9]{0,1:T(8,128)S(1)}) all-reduce(f32[9]{0:T(128)S(1)} %get-tuple-element.6, f32[9]{0:T(128)S(1)} %pad_add_fusion, f32[9,9]{0,1:T(8,128)S(1)} %fusion.18), channel_id=1, replica_groups=mesh['case'=8,'slab'=64] {'case','slab'}, use_global_device_ids=true, to_apply=%region_1.2 | all-reduce | flops 99 | bytes 792 | tf_op jit(solution)/shard_map/psum | solution.py:177
  133.7 0.8 cholesky.74
  137.2 0.7 fusion.98
  201.9 0.9 fusion.59
  202.8 0.9 fusion.57
  205.8 1.8 fusion.13
  207.6 99.6 %all-reduce.3 = (f32[9]{0:T(128)S(1)}, f32[9,9]{0,1:T(8,128)S(1)}) all-reduce(f32[9]{0:T(128)S(1)} %add_reduce_fusion.2, f32[9,9]{0,1:T(8,128)S(1)} %fusion.13), channel_id=1, replica_groups=mesh['case'=8,'slab'=64] {'case','slab'}, use_global_device_ids=true, to_apply=%region_11.13 | all-reduce | flops 90 | bytes 720 | tf_op jit(solution)/shard_map/psum | solution.py:177
  308.8 0.8 cholesky.85
  312.3 0.7 fusion.95
  376.3 0.9 fusion.55
  377.2 0.9 fusion.53
  380.3 1.8 fusion.8
  382.1 100.6 %all-reduce.2 = (f32[9]{0:T(128)S(1)}, f32[9,9]{0,1:T(8,128)S(1)}) all-reduce(f32[9]{0:T(128)S(1)} %add_reduce_fusion.1, f32[9,9]{0,1:T(8,128)S(1)} %fusion.8), channel_id=1, replica_groups=mesh['case'=8,'slab'=64] {'case','slab'}, use_global_device_ids=true, to_apply=%region_16.18 | all-reduce | flops 90 | bytes 720 | tf_op jit(solution)/shard_map/psum | solution.py:177
  484.2 0.8 cholesky.96
  487.7 0.7 fusion.92
  551.7 0.9 fusion.51
  552.6 0.9 fusion.49
  555.7 1.8 fusion.3
  557.5 99.6 %all-reduce.1 = (f32[9]{0:T(128)S(1)}, f32[9,9]{0,1:T(8,128)S(1)}) all-reduce(f32[9]{0:T(128)S(1)} %add_reduce_fusion, f32[9,9]{0,1:T(8,128)S(1)} %fusion.3), channel_id=1, replica_groups=mesh['case'=8,'slab'=64] {'case','slab'}, use_global_device_ids=true, to_apply=%region_21.23 | all-reduce | flops 90 | bytes 720 | tf_op jit(solution)/shard_map/psum | solution.py:177
  658.7 0.8 cholesky.107
  662.2 0.7 fusion.89
  726.2 0.9 fusion.47
  727.1 0.9 fusion.45
  (94 shorter events, 26.2 us)
Async XLA Ops:
  0.6 10.5 %copy-start.1 = (f32[1,1,16384]{2,1,0:T(1,128)S(1)}, f32[1,1,16384]{2,1,0:T(1,128)}, u32[]{:S(2)}) copy-start(f32[1,1,16384]{2,1,0:T(1,128)} %param.11) | copy-start | bytes 196612
  0.6 10.5 %copy-start.4 = (f32[1,1,16384]{2,1,0:T(1,128)S(1)}, f32[1,1,16384]{2,1,0:T(1,128)}, u32[]{:S(2)}) copy-start(f32[1,1,16384]{2,1,0:T(1,128)} %param.12) | copy-start | bytes 196612
  0.7 10.4 %copy-start.5 = (f32[1,1,16384]{2,1,0:T(1,128)S(1)}, f32[1,1,16384]{2,1,0:T(1,128)}, u32[]{:S(2)}) copy-start(f32[1,1,16384]{2,1,0:T(1,128)} %param.13) | copy-start | bytes 196612
  0.7 10.4 %copy-start.6 = (f32[1,1,16384]{2,1,0:T(1,128)S(1)}, f32[1,1,16384]{2,1,0:T(1,128)}, u32[]{:S(2)}) copy-start(f32[1,1,16384]{2,1,0:T(1,128)} %param.15) | copy-start | bytes 196612
  0.7 19.9 %all-to-all-start = ((f32[1,8,16384]{2,0,1:T(1,128)}), f32[1,8,16384]{2,0,1:T(1,128)S(1)}, u32[]{:S(2)}, u32[]{:S(2)}) async-start(f32[1,8,16384]{2,0,1:T(1,128)} %bitcast.360), calls=%async_computation | async-start | bytes 1048576 | tf_op jit(solution)/shard_map/all_to_all | solution.py:145
  11.1 0.9 copy-start.3
  12.0 0.8 copy-start.8
  12.0 2.0 copy-start
  131.5 0.7 copy-start.2
  138.0 0.7 copy-start.7
  726.2 0.9 copy-start.9
where the time goes:
time: 733 us; the launch traced here: 729 us
  blocking collectives  404 us (55%)
  between operations  256 us (35%)
  other arithmetic  22.2 us (3%)
  matrix products  16.5 us (2%)
  local copies, waits for them, and re-layouts  13.4 us (2%)
  starting transfers between devices  10.4 us (1%)
    psum x4, blocking collectives, per_device(): lax.psum((grad_local, hess_local), ('case', 'slab'))  404 us
  transfers between devices with their start and end apart: 1, of which 1 were waited for; matrix products, arithmetic and copies ran while one was open for 0% of the time, Pallas kernels for 0%

commit v1 on v0

v1 whole, which is shorter than its diff:
```python
import functools

import jax
import jax.numpy as jnp
from jax import lax
from jax.experimental import pallas as pl
from jax.experimental.pallas import tpu as pltpu
from jax.sharding import Mesh
from jax.sharding import PartitionSpec as P

NEWTON = 4
PROX = 0.1
VOLFRAC = 0.4
N = 9
PAIRS = [(i, k) for i in range(N) for k in range(i + 1)]
GRAD_AT = len(PAIRS)
VOL_AT = GRAD_AT + N
LANES = 128
HIGHEST = lax.Precision.HIGHEST


def vmem():
    return pl.BlockSpec(memory_space=pltpu.VMEM)


def smem():
    return pl.BlockSpec(memory_space=pltpu.SMEM)


def total(rows):
    while rows.shape[0] > 8:
        half = rows.shape[0] // 2
        rows = rows[:half] + rows[half:]
    return jnp.sum(rows, 0, keepdims=True)


def spread(gathered, table_ref):
    sums = total(gathered)
    count = table_ref.shape[0]
    row = lax.broadcasted_iota(jnp.int32, (count, LANES), 0)
    lane = lax.broadcasted_iota(jnp.int32, (count, LANES), 1)
    diagonal = jnp.where(row == lane, sums, 0.0)
    table_ref[...] = jnp.dot(
        diagonal,
        jnp.ones((LANES, LANES), jnp.float32),
        precision=HIGHEST,
        preferred_element_type=jnp.float32,
    )


def solve(matrix, vector):
    m = dict(matrix)
    b = list(vector)
    inverse = []
    for k in range(N):
        r = 1.0 / m[k, k]
        inverse.append(r)
        for i in range(k + 1, N):
            scaled = m[i, k] * r
            for j in range(k + 1, i + 1):
                m[i, j] = m[i, j] - scaled * m[j, k]
            b[i] = b[i] - scaled * b[k]
    x = [None] * N
    for k in reversed(range(N)):
        running = b[k]
        for i in range(k + 1, N):
            running = running - m[i, k] * x[i]
        x[k] = running * inverse[k]
    return x


def newton(table_ref, duals, volume, case_values_ref, element_total):
    scale = 1.0 / element_total
    excess = functools.reduce(jnp.add, duals[:-1]) - 1.0
    height = jnp.maximum(excess, 0.0)
    active = jnp.where(excess > 0, 1.0, 0.0)
    matrix = {}
    for at, (i, k) in enumerate(PAIRS):
        entry = table_ref[at : at + 1, :] * scale
        if i < N - 1:
            entry = entry + active
        matrix[i, k] = entry
    trace = functools.reduce(jnp.add, [matrix[i, i] for i in range(N)])
    damping = trace * (0.5 / N) + 0.0001
    vector = []
    for i in range(N):
        matrix[i, i] = matrix[i, i] + damping
        entry = table_ref[GRAD_AT + i : GRAD_AT + i + 1, :] * scale
        if i < N - 1:
            entry = entry + case_values_ref[i] - height
        else:
            entry = entry + volume - VOLFRAC
        vector.append(entry)
    step = solve(matrix, vector)
    return [jnp.maximum(l + d, 0.1 * l) for l, d in zip(duals, step)]


def place(duals, ups, downs, a, b, lo, hi):
    p = functools.reduce(jnp.add, [l * u for l, u in zip(duals, ups)]) + PROX
    q = functools.reduce(jnp.add, [l * d for l, d in zip(duals, downs)]) + PROX
    root_p = jnp.sqrt(p)
    root_q = jnp.sqrt(q)
    free = a * b * (root_q - root_p) / (a * root_p + b * root_q)
    return p, q, free, jnp.minimum(jnp.maximum(free, lo), hi)


def evaluate(duals, up_ref, down_ref, aux_ref, scaled_ref, stat_ref):
    steps = aux_ref.shape[1] // 8
    duals = [jnp.broadcast_to(l, (8, LANES)) for l in duals]

    def column(j, grads):
        rows = pl.ds(pl.multiple_of(j * 8, 8), 8)
        a, b, lo, hi = (aux_ref[k, rows, :] for k in range(4))
        ups = [up_ref[i, rows, :] for i in range(N)]
        downs = [down_ref[i, rows, :] for i in range(N)]
        p, q, free, t = place(duals, ups, downs, a, b, lo, hi)
        inside = (free > lo) & (free < hi)
        ru = 1.0 / (a - t)
        rl = 1.0 / (b + t)
        up_at = a * ru
        down_at = b * rl
        up_two = up_at * up_at
        down_two = down_at * down_at
        curve = 2.0 * (p * up_two * ru + q * down_two * rl)
        root = jnp.where(inside, lax.rsqrt(curve), 0.0)
        cu, cd = up_two * root, down_two * root
        tu, td = t * up_at, t * down_at
        out = []
        for i in range(N):
            scaled_ref[i, rows, :] = cu * ups[i] - cd * downs[i]
            out.append(grads[i] + (tu * ups[i] - td * downs[i]))
        return tuple(out)

    zero = jnp.zeros((8, LANES), jnp.float32)
    grads = lax.fori_loop(0, steps, column, (zero,) * N)
    for i in range(N):
        stat_ref[GRAD_AT + i : GRAD_AT + i + 1, :] = jnp.sum(grads[i], 0, keepdims=True)
    groups = [(0, 3), (3, 6), (6, 9)]
    for at, (i0, i1) in enumerate(groups):
        for k0, k1 in groups[: at + 1]:
            pairs = [(i, k) for i in range(i0, i1) for k in range(k0, min(k1, i + 1))]

            def products(j, sums, pairs=pairs):
                rows = pl.ds(pl.multiple_of(j * 8, 8), 8)
                held = {i: scaled_ref[i, rows, :] for i in sorted({i for pair in pairs for i in pair})}
                return tuple(s + held[i] * held[k] for s, (i, k) in zip(sums, pairs))

            sums = lax.fori_loop(0, steps, products, (zero,) * len(pairs), unroll=4)
            for s, pair in zip(sums, pairs):
                row = PAIRS.index(pair)
                stat_ref[row : row + 1, :] = jnp.sum(s, 0, keepdims=True)


def announce(stat_ref, message_ref):
    sums = lax.dot_general(
        jnp.ones((8, LANES), jnp.float32),
        stat_ref[...],
        (((1,), (1,)), ((), ())),
        precision=HIGHEST,
        preferred_element_type=jnp.float32,
    )
    for at in range(0, message_ref.shape[0], 8):
        message_ref[at : at + 8, :] = sums


def first_kernel(
    duals_ref, g_ref, x_ref, x1_ref, x2_ref, gl_ref, gu_ref, w_ref,
    lower_ref, upper_ref, up_ref, down_ref, aux_ref, state_ref, message_ref,
    scaled_ref, stat_ref,
):
    steps = x_ref.shape[0] // 8

    def column(j, volume):
        rows = pl.ds(pl.multiple_of(j * 8, 8), 8)
        x, x1, x2, w = (r[rows, :] for r in (x_ref, x1_ref, x2_ref, w_ref))
        trend = (x - x1) * (x1 - x2)
        factor = jnp.where(trend > 0, 1.2, jnp.where(trend < 0, 0.7, 1.0))
        lower = jnp.minimum(x - factor * gl_ref[rows, :], x - 0.01)
        upper = jnp.maximum(x + factor * gu_ref[rows, :], x + 0.01)
        lower_ref[rows, :] = lower
        upper_ref[rows, :] = upper
        a = upper - x
        b = x - lower
        aux_ref[0, rows, :] = a
        aux_ref[1, rows, :] = b
        aux_ref[2, rows, :] = jnp.maximum(jnp.maximum(lower + 0.1 * b, x - 0.2), 0.0) - x
        aux_ref[3, rows, :] = jnp.minimum(jnp.minimum(upper - 0.1 * a, x + 0.2), 1.0) - x
        for i in range(N):
            g = g_ref[i, rows, :] if i < N - 1 else w
            up_ref[i, rows, :] = jnp.maximum(1.001 * g, -0.001 * g)
            down_ref[i, rows, :] = jnp.maximum(0.001 * g, -1.001 * g)
        return volume + w * x

    volume = lax.fori_loop(0, steps, column, jnp.zeros((8, LANES), jnp.float32))
    stat_ref[VOL_AT:, :] = jnp.zeros((LANES - VOL_AT, LANES), jnp.float32)
    stat_ref[VOL_AT : VOL_AT + 1, :] = jnp.sum(volume, 0, keepdims=True)
    duals = [jnp.full((1, LANES), duals_ref[i], jnp.float32) for i in range(N)]
    state_ref[...] = jnp.zeros(state_ref.shape, jnp.float32)
    for i in range(N):
        state_ref[i : i + 1, :] = duals[i]
    evaluate(duals, up_ref, down_ref, aux_ref, scaled_ref, stat_ref)
    announce(stat_ref, message_ref)


def update(element_total, case_values_ref, gathered_ref, state_ref, table_ref):
    spread(gathered_ref[...], table_ref)
    duals = [state_ref[i : i + 1, :] for i in range(N)]
    volume = state_ref[N : N + 1, :] + table_ref[VOL_AT : VOL_AT + 1, :] * (1.0 / element_total)
    return newton(table_ref, duals, volume, case_values_ref, element_total), volume


def middle_kernel(
    element_total,
    case_values_ref, gathered_ref, state_ref, up_ref, down_ref, aux_ref,
    new_state_ref, message_ref,
    scaled_ref, stat_ref, table_ref,
):
    duals, volume = update(element_total, case_values_ref, gathered_ref, state_ref, table_ref)
    new_state_ref[...] = jnp.zeros(new_state_ref.shape, jnp.float32)
    for i in range(N):
        new_state_ref[i : i + 1, :] = duals[i]
    new_state_ref[N : N + 1, :] = volume
    stat_ref[VOL_AT:, :] = jnp.zeros((LANES - VOL_AT, LANES), jnp.float32)
    evaluate(duals, up_ref, down_ref, aux_ref, scaled_ref, stat_ref)
    announce(stat_ref, message_ref)


def last_kernel(
    element_total,
    case_values_ref, gathered_ref, state_ref, up_ref, down_ref, aux_ref, x_ref,
    design_ref, duals_ref,
    table_ref,
):
    duals, _ = update(element_total, case_values_ref, gathered_ref, state_ref, table_ref)
    lane = lax.broadcasted_iota(jnp.int32, (1, LANES), 1)
    row = jnp.zeros((1, LANES), jnp.float32)
    for i in range(N):
        row = jnp.where(lane == i, duals[i], row)
    duals_ref[...] = row
    wide = [jnp.broadcast_to(l, (8, LANES)) for l in duals]

    def column(j, carry):
        rows = pl.ds(pl.multiple_of(j * 8, 8), 8)
        a, b, lo, hi = (aux_ref[k, rows, :] for k in range(4))
        ups = [up_ref[i, rows, :] for i in range(N)]
        downs = [down_ref[i, rows, :] for i in range(N)]
        _, _, _, t = place(wide, ups, downs, a, b, lo, hi)
        design_ref[rows, :] = x_ref[rows, :] + t
        return carry

    lax.fori_loop(0, aux_ref.shape[1] // 8, column, 0)


def f32(*shape):
    return jax.ShapeDtypeStruct(shape, jnp.float32)


PARAMS = pltpu.CompilerParams(vmem_limit_bytes=16 * 1024 * 1024)
NEAR = ("x", "y")
FAR = ("core", "z")


def per_device(sensitivity, x, x1, x2, gl, gu, w, case_values, duals_start):
    sizes = {name: lax.axis_size(name) for name in ("x", "core", "y", "z")}
    near = sizes["x"] * sizes["y"]
    far = sizes["core"] * sizes["z"]
    cases = sizes["x"] * sizes["core"]
    depth = x.size // LANES
    element_total = float(x.size * near * far)
    shape = x.shape
    x, x1, x2, gl, gu, w = (v.reshape(depth, LANES) for v in (x, x1, x2, gl, gu, w))
    g = lax.all_to_all(
        sensitivity.reshape(cases, depth, LANES), ("x", "core"), split_axis=0, concat_axis=0, tiled=True
    )

    def gather(message):
        heard = lax.all_to_all(message, NEAR, split_axis=0, concat_axis=0, tiled=True)
        part = jnp.broadcast_to(jnp.sum(heard, 0, keepdims=True), (far, LANES))
        return lax.all_to_all(part, FAR, split_axis=0, concat_axis=0, tiled=True)

    lower, upper, up, down, aux, state, message = pl.pallas_call(
        first_kernel,
        out_shape=(
            f32(depth, LANES), f32(depth, LANES), f32(N, depth, LANES), f32(N, depth, LANES),
            f32(4, depth, LANES), f32(16, LANES), f32(near, LANES),
        ),
        in_specs=[smem()] + [vmem()] * 7,
        out_specs=(vmem(),) * 7,
        scratch_shapes=[pltpu.VMEM((N, depth, LANES), jnp.float32), pltpu.VMEM((LANES, LANES), jnp.float32)],
        compiler_params=PARAMS,
    )(duals_start, g, x, x1, x2, gl, gu, w)
    for _ in range(NEWTON - 1):
        state, message = pl.pallas_call(
            functools.partial(middle_kernel, element_total),
            out_shape=(f32(16, LANES), f32(near, LANES)),
            in_specs=[smem()] + [vmem()] * 5,
            out_specs=(vmem(),) * 2,
            scratch_shapes=[
                pltpu.VMEM((N, depth, LANES), jnp.float32),
                pltpu.VMEM((LANES, LANES), jnp.float32),
                pltpu.VMEM((64, LANES), jnp.float32),
            ],
            compiler_params=PARAMS,
        )(case_values, gather(message), state, up, down, aux)
    design, duals = pl.pallas_call(
        functools.partial(last_kernel, element_total),
        out_shape=(f32(depth, LANES), f32(1, LANES)),
        in_specs=[smem()] + [vmem()] * 6,
        out_specs=(vmem(),) * 2,
        scratch_shapes=[pltpu.VMEM((64, LANES), jnp.float32)],
        compiler_params=PARAMS,
    )(case_values, gather(message), state, up, down, aux, x)
    return design.reshape(shape), lower.reshape(shape), upper.reshape(shape), duals[0, :N]


def solution(mesh):
    cases, slabs = mesh.devices.shape
    fine = Mesh(mesh.devices.reshape(cases // 2, 2, 4, slabs // 4), ("x", "core", "y", "z"))
    case, slab = ("x", "core"), ("y", "z")
    design = P(slab, case, None)
    return jax.shard_map(
        per_device,
        mesh=fine,
        in_specs=(P(case, slab),) + (design,) * 6 + (P(), P()),
        out_specs=(design, design, design, P()),
        check_vma=False,
    )
```

time: 733 us -> 148 us (0.20)
  blocking collectives: 404 us -> 133 us
  between operations: 256 us -> 0.72 us
  other arithmetic: 22.2 us -> 0.14 us
  matrix products: 16.5 us -> 0 us
  Pallas kernels: 0 us -> 12.1 us
  local copies, waits for them, and re-layouts: 13.4 us -> 1.86 us
  starting transfers between devices: 10.4 us -> 0 us
    psum x4 -> x0, blocking collectives: 404 us -> none  [per_device(): lax.psum((grad_local, hess_local), ('case', 'slab'))]
    all_to_all x0 -> x9, blocking collectives: none -> 133 us  [the longest x4 76.5 us: gather(): return lax.all_to_all(part, FAR, split_axis=0, concat_axis=0, tiled=True)]
    dot_general x14 -> x0, matrix products: 16.5 us -> none  [the longest x4 7.26 us: evaluate(): hessian = jnp.dot(scaled, scaled.T, precision=lax.Precision.HIGHEST)]
    pallas_call x0 -> x5, Pallas kernels: none -> 12.1 us  [the longest x3 7.24 us: per_device(): pl.pallas_call(functools.partial(middle_kernel, element_total), out_shape...]
    slice x16 -> x0, local copies, waits for them, and re-layouts: 11.1 us -> none  [the longest x4 2.91 us: solve_small(): forward.append(running / factor_l[row_at, row_at])]
    all_to_all x1 -> x0, starting transfers between devices: 10.4 us -> none  [per_device(): lax.all_to_all(sensitivity.reshape(owned, case_count, piece), 'case', spl...]
    reduce_sum x12 -> x4, other arithmetic: 8.23 us -> 0.14 us  [gather(): part = jnp.broadcast_to(jnp.sum(heard, 0, keepdims=True), (far, LANES))]
  transfers between devices with their start and end apart: 1 -> 0, of which waited for: 1 -> 0; matrix products, arithmetic and copies ran while one was open for 0% -> 0% of each run, Pallas kernels for 0% -> 0%
where the time goes in v1:
time: 148 us
  blocking collectives  133 us (90%)
  Pallas kernels  12.1 us (8%)
  local copies, waits for them, and re-layouts  1.86 us (1%)
    all_to_all x4, blocking collectives, gather(): return lax.all_to_all(part, FAR, split_axis=0, concat_axis=0, tiled=True)  76.5 us
    all_to_all x4, blocking collectives, gather(): lax.all_to_all(message, NEAR, split_axis=0, concat_axis=0, tiled=True)  36.5 us
    all_to_all x1, blocking collectives, per_device(): lax.all_to_all(sensitivity.reshape(cases, depth, LANES), ('x', 'core'), s...  19.8 us
    pallas_call x3, Pallas kernels, per_device(): pl.pallas_call(functools.partial(middle_kernel, element_total), out_shape...  7.24 us

profile of v1, /device:TPU:1, one launch (start us, length us, event | category | flops | bytes accessed | tf_op | source)
XLA Modules:
  0.0 147.7 jit_solution(18091050224353250832)
XLA Ops:
  0.6 0.0 copy-start
  0.6 0.0 copy-start.1
  0.7 0.0 copy-start.2
  0.7 0.0 copy-start.3
  0.7 0.0 copy-start.4
  0.7 0.0 copy-start.5
  0.7 19.8 %all_to_all.73.g_ref = f32[8,128,128]{2,1,0:T(8,128)S(1)} all-to-all(f32[8,128,128]{2,1,0:T(8,128)} %bitcast.43), channel_id=1, replica_groups=mesh['x'=4,'core'=2,'y'=4,'z'=16] {'x','core'}, dimensions={0} | all-to-all | bytes 1048576 | tf_op jit(solution)/shard_map/all_to_all | solution.py:272
  20.5 0.0 copy-start.7
  20.5 0.0 copy-done
  20.5 0.0 copy-done.1
  20.5 0.0 copy-done.2
  20.5 0.0 copy-done.3
  20.5 0.0 copy-done.4
  20.5 0.0 copy-done.5
  20.5 0.6 copy-done.7
  21.1 2.8 %shard_map.120 = (f32[128,128]{1,0:T(8,128)}, f32[128,128]{1,0:T(8,128)}, f32[9,128,128]{2,1,0:T(8,128)S(1)}, f32[9,128,128]{2,1,0:T(8,128)S(1)}, f32[4,128,128]...) custom-call(f32[9]{0:T(128)S(1)} %copy-done.7, f32[8,128,128]{2,1,0:T(8,128)S(1)} %all_to_all.73.g_ref, ...), custom_call_target="tpu_custom_call" | custom-call | tf_op jit(solution)/shard_map/pallas_call | solution.py:281
  24.0 8.9 %all_to_all.74 = f32[16,1,128]{2,1,0:T(1,128)S(1)} all-to-all(f32[16,1,128]{2,1,0:T(1,128)S(1)} %bitcast.39), channel_id=1, replica_groups=mesh['x'=4,'core'=2,'y'=4,'z'=16] {'x','y'}, dimensions={0} | all-to-all | bytes 16384 | tf_op jit(solution)/shard_map/all_to_all | solution.py:277
  33.0 27.2 %all_to_all.75 = f32[32,1,128]{2,1,0:T(1,128)S(1)} all-to-all(f32[32,1,128]{2,1,0:T(1,128)S(1)} %broadcast_in_dim.8), channel_id=1, replica_groups=mesh['x'=4,'core'=2,'y'=4,'z'=16] {'core','z'}, dimensions={0} | all-to-all | bytes 32768 | tf_op jit(solution)/shard_map/all_to_all | solution.py:279
  60.1 0.0 copy-start.6
  60.1 0.7 copy-done.6
  60.8 2.4 %shard_map.121 = (f32[16,128]{1,0:T(8,128)S(1)}, f32[16,128]{1,0:T(8,128)S(1)}) custom-call(f32[8]{0:T(128)S(1)} %copy-done.6, f32[32,128]{1,0:T(8,128)S(1)} %bitcast.33, f32[16,128]{1,0:T(8,128)S(1)} %get-tuple-element.20.state_ref, f32[9,128,128]{2,1,0:T(8,128)S(1)} %get-tuple-element.21.up_ref, f32[9,128,128]{2,1,0:T(8,128)S(1)} %get-tuple-element.22.down_ref, ...), custom_call_target="tpu_custom_call" | custom-call | tf_op jit(solution)/shard_map/pallas_call | solution.py:293
  63.2 9.2 %all_to_all.76 = f32[16,1,128]{2,1,0:T(1,128)S(1)} all-to-all(f32[16,1,128]{2,1,0:T(1,128)S(1)} %bitcast.40), channel_id=1, replica_groups=mesh['x'=4,'core'=2,'y'=4,'z'=16] {'x','y'}, dimensions={0} | all-to-all | bytes 16384 | tf_op jit(solution)/shard_map/all_to_all | solution.py:277
  72.4 16.5 %all_to_all.77 = f32[32,1,128]{2,1,0:T(1,128)S(1)} all-to-all(f32[32,1,128]{2,1,0:T(1,128)S(1)} %broadcast_in_dim.9), channel_id=1, replica_groups=mesh['x'=4,'core'=2,'y'=4,'z'=16] {'core','z'}, dimensions={0} | all-to-all | bytes 32768 | tf_op jit(solution)/shard_map/all_to_all | solution.py:279
  88.9 2.4 %shard_map.122 = (f32[16,128]{1,0:T(8,128)S(1)}, f32[16,128]{1,0:T(8,128)S(1)}) custom-call(f32[8]{0:T(128)S(1)} %copy-done.6, f32[32,128]{1,0:T(8,128)S(1)} %bitcast.31, f32[16,128]{1,0:T(8,128)S(1)} %get-tuple-element.25.state_ref, f32[9,128,128]{2,1,0:T(8,128)S(1)} %get-tuple-element.21.up_ref, f32[9,128,128]{2,1,0:T(8,128)S(1)} %get-tuple-element.22.down_ref, ...), custom_call_target="tpu_custom_call" | custom-call | tf_op jit(solution)/shard_map/pallas_call | solution.py:293
  91.3 9.2 %all_to_all.78 = f32[16,1,128]{2,1,0:T(1,128)S(1)} all-to-all(f32[16,1,128]{2,1,0:T(1,128)S(1)} %bitcast.41), channel_id=1, replica_groups=mesh['x'=4,'core'=2,'y'=4,'z'=16] {'x','y'}, dimensions={0} | all-to-all | bytes 16384 | tf_op jit(solution)/shard_map/all_to_all | solution.py:277
  100.6 16.4 %all_to_all.79 = f32[32,1,128]{2,1,0:T(1,128)S(1)} all-to-all(f32[32,1,128]{2,1,0:T(1,128)S(1)} %broadcast_in_dim.10), channel_id=1, replica_groups=mesh['x'=4,'core'=2,'y'=4,'z'=16] {'core','z'}, dimensions={0} | all-to-all | bytes 32768 | tf_op jit(solution)/shard_map/all_to_all | solution.py:279
  117.0 2.4 %shard_map.123 = (f32[16,128]{1,0:T(8,128)S(1)}, f32[16,128]{1,0:T(8,128)S(1)}) custom-call(f32[8]{0:T(128)S(1)} %copy-done.6, f32[32,128]{1,0:T(8,128)S(1)} %bitcast.32, f32[16,128]{1,0:T(8,128)S(1)} %get-tuple-element.27.state_ref, f32[9,128,128]{2,1,0:T(8,128)S(1)} %get-tuple-element.21.up_ref, f32[9,128,128]{2,1,0:T(8,128)S(1)} %get-tuple-element.22.down_ref, ...), custom_call_target="tpu_custom_call" | custom-call | tf_op jit(solution)/shard_map/pallas_call | solution.py:293
  119.4 9.2 %all_to_all.80 = f32[16,1,128]{2,1,0:T(1,128)S(1)} all-to-all(f32[16,1,128]{2,1,0:T(1,128)S(1)} %bitcast.42), channel_id=1, replica_groups=mesh['x'=4,'core'=2,'y'=4,'z'=16] {'x','y'}, dimensions={0} | all-to-all | bytes 16384 | tf_op jit(solution)/shard_map/all_to_all | solution.py:277
  128.7 16.4 %all_to_all.81 = f32[32,1,128]{2,1,0:T(1,128)S(1)} all-to-all(f32[32,1,128]{2,1,0:T(1,128)S(1)} %broadcast_in_dim.11), channel_id=1, replica_groups=mesh['x'=4,'core'=2,'y'=4,'z'=16] {'core','z'}, dimensions={0} | all-to-all | bytes 32768 | tf_op jit(solution)/shard_map/all_to_all | solution.py:279
  145.1 2.1 %shard_map.124 = (f32[128,128]{1,0:T(8,128)}, f32[1,128]{1,0:T(1,128)S(1)}) custom-call(f32[8]{0:T(128)S(1)} %copy-done.6, f32[32,128]{1,0:T(8,128)S(1)} %bitcast.30, f32[16,128]{1,0:T(8,128)S(1)} %get-tuple-element.29.state_ref, f32[9,128,128]{2,1,0:T(8,128)S(1)} %get-tuple-element.21.up_ref, f32[9,128,128]{2,1,0:T(8,128)S(1)} %get-tuple-element.22.down_ref, ...), custom_call_target="tpu_custom_call" | custom-call | tf_op jit(solution)/shard_map/pallas_call | solution.py:305
  147.2 0.5 slice_bitcast_fusion
  (8 shorter events, 0.2 us)
Async XLA Ops:
  0.6 19.8 %copy-start = (f32[1,1,16384]{2,1,0:T(1,128)S(1)}, f32[1,1,16384]{2,1,0:T(1,128)}, u32[]{:S(2)}) copy-start(f32[1,1,16384]{2,1,0:T(1,128)} %param.10) | copy-start | bytes 196612
  0.6 19.8 %copy-start.1 = (f32[1,1,16384]{2,1,0:T(1,128)S(1)}, f32[1,1,16384]{2,1,0:T(1,128)}, u32[]{:S(2)}) copy-start(f32[1,1,16384]{2,1,0:T(1,128)} %param.11) | copy-start | bytes 196612
  0.7 19.8 %copy-start.2 = (f32[1,1,16384]{2,1,0:T(1,128)S(1)}, f32[1,1,16384]{2,1,0:T(1,128)}, u32[]{:S(2)}) copy-start(f32[1,1,16384]{2,1,0:T(1,128)} %param.12) | copy-start | bytes 196612
  0.7 19.8 %copy-start.3 = (f32[1,1,16384]{2,1,0:T(1,128)S(1)}, f32[1,1,16384]{2,1,0:T(1,128)}, u32[]{:S(2)}) copy-start(f32[1,1,16384]{2,1,0:T(1,128)} %param.13) | copy-start | bytes 196612
  0.7 19.8 %copy-start.4 = (f32[1,1,16384]{2,1,0:T(1,128)S(1)}, f32[1,1,16384]{2,1,0:T(1,128)}, u32[]{:S(2)}) copy-start(f32[1,1,16384]{2,1,0:T(1,128)} %param.14) | copy-start | bytes 196612
  0.7 19.8 %copy-start.5 = (f32[1,1,16384]{2,1,0:T(1,128)S(1)}, f32[1,1,16384]{2,1,0:T(1,128)}, u32[]{:S(2)}) copy-start(f32[1,1,16384]{2,1,0:T(1,128)} %param.15) | copy-start | bytes 196612
  20.5 0.7 copy-start.7
  60.1 0.7 copy-start.6

commit v2 on v1

v2 whole, which is shorter than its diff:
```python
import functools

import jax
import jax.numpy as jnp
from jax import lax
from jax.experimental import pallas as pl
from jax.experimental.pallas import tpu as pltpu
from jax.sharding import Mesh
from jax.sharding import PartitionSpec as P

NEWTON = 4
PROX = 0.1
VOLFRAC = 0.4
N = 9
PAIRS = [(i, k) for i in range(N) for k in range(i + 1)]
GRAD_AT = len(PAIRS)
VOL_AT = GRAD_AT + N
LANES = 128
TARGET_AT = 16
STATE = 32
CHUNK = 32
KUNROLL = 16
HIGHEST = lax.Precision.HIGHEST


def vmem():
    return pl.BlockSpec(memory_space=pltpu.VMEM)


def total(rows):
    while rows.shape[0] > 8:
        half = rows.shape[0] // 2
        rows = rows[:half] + rows[half:]
    return jnp.sum(rows, 0, keepdims=True)


def spread(gathered, table_ref):
    sums = total(gathered)
    count = table_ref.shape[0]
    row = lax.broadcasted_iota(jnp.int32, (count, LANES), 0)
    lane = lax.broadcasted_iota(jnp.int32, (count, LANES), 1)
    diagonal = jnp.where(row == lane, sums, 0.0)
    table_ref[...] = jnp.dot(
        diagonal,
        jnp.ones((LANES, LANES), jnp.float32),
        precision=HIGHEST,
        preferred_element_type=jnp.float32,
    )


def solve(matrix, vector):
    m = dict(matrix)
    b = list(vector)
    inverse = []
    for k in range(N):
        r = 1.0 / m[k, k]
        inverse.append(r)
        for i in range(k + 1, N):
            scaled = m[i, k] * r
            for j in range(k + 1, i + 1):
                m[i, j] = m[i, j] - scaled * m[j, k]
            b[i] = b[i] - scaled * b[k]
    x = [None] * N
    for k in reversed(range(N)):
        running = b[k]
        for i in range(k + 1, N):
            running = running - m[i, k] * x[i]
        x[k] = running * inverse[k]
    return x


def newton(table_ref, duals, targets, element_total):
    scale = 1.0 / element_total
    excess = functools.reduce(jnp.add, duals[:-1]) - 1.0
    height = jnp.maximum(excess, 0.0)
    active = jnp.where(excess > 0, 1.0, 0.0)
    matrix = {}
    for at, (i, k) in enumerate(PAIRS):
        entry = table_ref[at : at + 1, :] * scale
        if i < N - 1:
            entry = entry + active
        matrix[i, k] = entry
    trace = functools.reduce(jnp.add, [matrix[i, i] for i in range(N)])
    damping = trace * (0.5 / N) + 0.0001
    vector = []
    for i in range(N):
        matrix[i, i] = matrix[i, i] + damping
        entry = table_ref[GRAD_AT + i : GRAD_AT + i + 1, :] * scale + targets[i]
        vector.append(entry - height if i < N - 1 else entry)
    step = solve(matrix, vector)
    return [jnp.maximum(l + d, 0.1 * l) for l, d in zip(duals, step)]


def place(duals, ups, downs, a, b, lo, hi):
    p = functools.reduce(jnp.add, [l * u for l, u in zip(duals, ups)]) + PROX
    q = functools.reduce(jnp.add, [l * d for l, d in zip(duals, downs)]) + PROX
    root_p = jnp.sqrt(p)
    root_q = jnp.sqrt(q)
    free = a * b * (root_q - root_p) / (a * root_p + b * root_q)
    return p, q, free, jnp.minimum(jnp.maximum(free, lo), hi)


def evaluate(duals, up_ref, down_ref, aux_ref, scaled_ref, stat_ref, before=None):
    depth = aux_ref.shape[1]
    duals = [jnp.broadcast_to(l, (CHUNK, LANES)) for l in duals]

    def fold(v):
        return jnp.sum(v.reshape(-1, 8, LANES), 0)

    def column(j, grads):
        rows = pl.ds(pl.multiple_of(j * CHUNK, CHUNK), CHUNK)
        if before is not None:
            before(rows)
        a, b, lo, hi = (aux_ref[k, rows, :] for k in range(4))
        ups = [up_ref[i, rows, :] for i in range(N)]
        downs = [down_ref[i, rows, :] for i in range(N)]
        p, q, free, t = place(duals, ups, downs, a, b, lo, hi)
        inside = (free > lo) & (free < hi)
        ru = 1.0 / (a - t)
        rl = 1.0 / (b + t)
        up_at = a * ru
        down_at = b * rl
        up_two = up_at * up_at
        down_two = down_at * down_at
        curve = 2.0 * (p * up_two * ru + q * down_two * rl)
        root = jnp.where(inside, lax.rsqrt(curve), 0.0)
        cu, cd = up_two * root, down_two * root
        tu, td = t * up_at, t * down_at
        out = []
        for i in range(N):
            scaled_ref[i, rows, :] = cu * ups[i] - cd * downs[i]
            out.append(grads[i] + fold(tu * ups[i] - td * downs[i]))
        return tuple(out)

    zero = jnp.zeros((8, LANES), jnp.float32)
    grads = lax.fori_loop(0, depth // CHUNK, column, (zero,) * N)
    for i in range(N):
        stat_ref[GRAD_AT + i : GRAD_AT + i + 1, :] = jnp.sum(grads[i], 0, keepdims=True)
    groups = [(0, 3), (3, 6), (6, 9)]
    for at, (i0, i1) in enumerate(groups):
        for k0, k1 in groups[: at + 1]:
            pairs = [(i, k) for i in range(i0, i1) for k in range(k0, min(k1, i + 1))]

            def products(j, sums, pairs=pairs):
                rows = pl.ds(pl.multiple_of(j * 8, 8), 8)
                held = {i: scaled_ref[i, rows, :] for i in sorted({i for pair in pairs for i in pair})}
                return tuple(s + held[i] * held[k] for s, (i, k) in zip(sums, pairs))

            sums = lax.fori_loop(0, depth // 8, products, (zero,) * len(pairs), unroll=KUNROLL)
            for s, pair in zip(sums, pairs):
                row = PAIRS.index(pair)
                stat_ref[row : row + 1, :] = jnp.sum(s, 0, keepdims=True)


def announce(stat_ref, message_ref):
    sums = lax.dot_general(
        jnp.ones((8, LANES), jnp.float32),
        stat_ref[...],
        (((1,), (1,)), ((), ())),
        precision=HIGHEST,
        preferred_element_type=jnp.float32,
    )
    for at in range(0, message_ref.shape[0], 8):
        message_ref[at : at + 8, :] = sums


def prepare_kernel(
    duals_ref, case_values_ref, x_ref, x1_ref, x2_ref, gl_ref, gu_ref, w_ref,
    lower_ref, upper_ref, aux_ref, volume_ref, state_ref,
):
    x, x1, x2, w = (r[...] for r in (x_ref, x1_ref, x2_ref, w_ref))
    trend = (x - x1) * (x1 - x2)
    factor = jnp.where(trend > 0, 1.2, jnp.where(trend < 0, 0.7, 1.0))
    lower = jnp.minimum(x - factor * gl_ref[...], x - 0.01)
    upper = jnp.maximum(x + factor * gu_ref[...], x + 0.01)
    lower_ref[...] = lower
    upper_ref[...] = upper
    a = upper - x
    b = x - lower
    aux_ref[0] = a
    aux_ref[1] = b
    aux_ref[2] = jnp.maximum(jnp.maximum(lower + 0.1 * b, x - 0.2), 0.0) - x
    aux_ref[3] = jnp.minimum(jnp.minimum(upper - 0.1 * a, x + 0.2), 1.0) - x
    volume_ref[...] = jnp.sum((w * x).reshape(-1, 8, LANES), 0)
    state_ref[...] = jnp.zeros(state_ref.shape, jnp.float32)
    for i in range(N):
        state_ref[i : i + 1, :] = jnp.broadcast_to(duals_ref[0:1, i : i + 1], (1, LANES))
    for i in range(N - 1):
        state_ref[TARGET_AT + i : TARGET_AT + i + 1, :] = jnp.broadcast_to(
            case_values_ref[0:1, i : i + 1], (1, LANES)
        )
    state_ref[TARGET_AT + N - 1 : TARGET_AT + N, :] = jnp.full((1, LANES), -VOLFRAC)


def first_kernel(
    g_ref, w_ref, aux_ref, volume_ref, state_ref,
    up_ref, down_ref, message_ref,
    scaled_ref, stat_ref,
):
    def slopes(rows):
        for i in range(N):
            g = g_ref[i, rows, :] if i < N - 1 else w_ref[rows, :]
            up_ref[i, rows, :] = jnp.maximum(1.001 * g, -0.001 * g)
            down_ref[i, rows, :] = jnp.maximum(0.001 * g, -1.001 * g)

    stat_ref[VOL_AT:, :] = jnp.zeros((LANES - VOL_AT, LANES), jnp.float32)
    stat_ref[VOL_AT : VOL_AT + 1, :] = jnp.sum(volume_ref[...], 0, keepdims=True)
    duals = [state_ref[i : i + 1, :] for i in range(N)]
    evaluate(duals, up_ref, down_ref, aux_ref, scaled_ref, stat_ref, slopes)
    announce(stat_ref, message_ref)


def update(element_total, gathered_ref, state_ref, table_ref):
    spread(gathered_ref[...], table_ref)
    duals = [state_ref[i : i + 1, :] for i in range(N)]
    targets = [state_ref[TARGET_AT + i : TARGET_AT + i + 1, :] for i in range(N)]
    targets[-1] = targets[-1] + table_ref[VOL_AT : VOL_AT + 1, :] * (1.0 / element_total)
    return newton(table_ref, duals, targets, element_total), targets


def middle_kernel(
    element_total,
    gathered_ref, state_ref, up_ref, down_ref, aux_ref,
    new_state_ref, message_ref,
    scaled_ref, stat_ref, table_ref,
):
    duals, targets = update(element_total, gathered_ref, state_ref, table_ref)
    new_state_ref[...] = state_ref[...]
    for i in range(N):
        new_state_ref[i : i + 1, :] = duals[i]
    new_state_ref[TARGET_AT + N - 1 : TARGET_AT + N, :] = targets[-1]
    stat_ref[VOL_AT:, :] = jnp.zeros((LANES - VOL_AT, LANES), jnp.float32)
    evaluate(duals, up_ref, down_ref, aux_ref, scaled_ref, stat_ref)
    announce(stat_ref, message_ref)


def last_kernel(
    element_total,
    gathered_ref, state_ref, up_ref, down_ref, aux_ref, x_ref,
    design_ref, duals_ref,
    table_ref,
):
    duals, _ = update(element_total, gathered_ref, state_ref, table_ref)
    lane = lax.broadcasted_iota(jnp.int32, (1, LANES), 1)
    row = jnp.zeros((1, LANES), jnp.float32)
    for i in range(N):
        row = jnp.where(lane == i, duals[i], row)
    duals_ref[...] = row[:, : duals_ref.shape[1]]
    wide = [jnp.broadcast_to(l, (CHUNK, LANES)) for l in duals]

    def column(j, carry):
        rows = pl.ds(pl.multiple_of(j * CHUNK, CHUNK), CHUNK)
        a, b, lo, hi = (aux_ref[k, rows, :] for k in range(4))
        ups = [up_ref[i, rows, :] for i in range(N)]
        downs = [down_ref[i, rows, :] for i in range(N)]
        _, _, _, t = place(wide, ups, downs, a, b, lo, hi)
        design_ref[rows, :] = x_ref[rows, :] + t
        return carry

    lax.fori_loop(0, aux_ref.shape[1] // CHUNK, column, 0)


def f32(*shape):
    return jax.ShapeDtypeStruct(shape, jnp.float32)


PARAMS = pltpu.CompilerParams(vmem_limit_bytes=16 * 1024 * 1024)
NEAR = ("x", "y")
FAR = ("core", "z")


def per_device(sensitivity, x, x1, x2, gl, gu, w, case_values, duals_start):
    sizes = {name: lax.axis_size(name) for name in ("x", "core", "y", "z")}
    near = sizes["x"] * sizes["y"]
    far = sizes["core"] * sizes["z"]
    cases = sizes["x"] * sizes["core"]
    depth = x.size // LANES
    element_total = float(x.size * near * far)
    shape = x.shape
    x, x1, x2, gl, gu, w = (v.reshape(depth, LANES) for v in (x, x1, x2, gl, gu, w))
    g = lax.all_to_all(
        sensitivity.reshape(cases, depth, LANES), ("x", "core"), split_axis=0, concat_axis=0, tiled=True
    )

    def gather(message):
        heard = lax.all_to_all(message, NEAR, split_axis=0, concat_axis=0, tiled=True)
        part = jnp.broadcast_to(jnp.sum(heard, 0, keepdims=True), (far, LANES))
        return lax.all_to_all(part, FAR, split_axis=0, concat_axis=0, tiled=True)

    lower, upper, aux, volume, state = pl.pallas_call(
        prepare_kernel,
        out_shape=(
            f32(depth, LANES), f32(depth, LANES), f32(4, depth, LANES), f32(8, LANES), f32(STATE, LANES),
        ),
        in_specs=[vmem()] * 8,
        out_specs=(vmem(),) * 5,
        compiler_params=PARAMS,
        cost_estimate=pl.CostEstimate(flops=10_000_000_000, bytes_accessed=40_000_000, transcendentals=0),
    )(duals_start.reshape(1, -1), case_values.reshape(1, -1), x, x1, x2, gl, gu, w)
    work = [pltpu.VMEM((N, depth, LANES), jnp.float32), pltpu.VMEM((LANES, LANES), jnp.float32)]
    table = [pltpu.VMEM((64, LANES), jnp.float32)]
    up, down, message = pl.pallas_call(
        first_kernel,
        out_shape=(f32(N, depth, LANES), f32(N, depth, LANES), f32(near, LANES)),
        in_specs=[vmem()] * 5,
        out_specs=(vmem(),) * 3,
        scratch_shapes=work,
        compiler_params=PARAMS,
    )(g, w, aux, volume, state)
    for _ in range(NEWTON - 1):
        state, message = pl.pallas_call(
            functools.partial(middle_kernel, element_total),
            out_shape=(f32(STATE, LANES), f32(near, LANES)),
            in_specs=[vmem()] * 5,
            out_specs=(vmem(),) * 2,
            scratch_shapes=work + table,
            compiler_params=PARAMS,
        )(gather(message), state, up, down, aux)
    design, duals = pl.pallas_call(
        functools.partial(last_kernel, element_total),
        out_shape=(f32(depth, LANES), f32(1, N)),
        in_specs=[vmem()] * 6,
        out_specs=(vmem(),) * 2,
        scratch_shapes=table,
        compiler_params=PARAMS,
    )(gather(message), state, up, down, aux, x)
    return design.reshape(shape), lower.reshape(shape), upper.reshape(shape), duals.reshape(N)


def solution(mesh):
    cases, slabs = mesh.devices.shape
    fine = Mesh(mesh.devices.reshape(cases // 2, 2, 4, slabs // 4), ("x", "core", "y", "z"))
    case, slab = ("x", "core"), ("y", "z")
    design = P(slab, case, None)
    return jax.shard_map(
        per_device,
        mesh=fine,
        in_specs=(P(case, slab),) + (design,) * 6 + (P(), P()),
        out_specs=(design, design, design, P()),
        check_vma=False,
    )
```

time: 148 us -> 140 us (0.946)
  blocking collectives: 133 us -> 113 us
  starting transfers between devices: 0 us -> 10.4 us
  waiting for transfers between devices: 0 us -> 8.13 us
  Pallas kernels: 12.1 us -> 6.47 us
    all_to_all x1 -> x0, blocking collectives: 19.8 us -> none  [per_device(): lax.all_to_all(sensitivity.reshape(cases, depth, LANES), ('x', 'core'), s...]
    all_to_all x0 -> x1, starting transfers between devices: none -> 10.4 us  [per_device(): lax.all_to_all(sensitivity.reshape(cases, depth, LANES), ('x', 'core'), s...]
    all_to_all x0 -> x1, waiting for transfers between devices: none -> 8.13 us  [per_device(): lax.all_to_all(sensitivity.reshape(cases, depth, LANES), ('x', 'core'), s...]
    pallas_call x3, Pallas kernels: 7.24 us -> 3.6 us  [per_device(): pl.pallas_call(functools.partial(middle_kernel, element_total), out_shape...]
  transfers between devices with their start and end apart: 0 -> 1, of which waited for: 0 -> 1; matrix products, arithmetic and copies ran while one was open for 0% -> 0% of each run, Pallas kernels for 0% -> 0%
where the time goes in v2:
time: 140 us; the launch traced here: 139 us
  blocking collectives  113 us (81%)
  starting transfers between devices  10.4 us (7%)
  waiting for transfers between devices  8.13 us (6%)
  Pallas kernels  6.47 us (5%)
    all_to_all x4, blocking collectives, gather(): return lax.all_to_all(part, FAR, split_axis=0, concat_axis=0, tiled=True)  76.4 us
    all_to_all x4, blocking collectives, gather(): lax.all_to_all(message, NEAR, split_axis=0, concat_axis=0, tiled=True)  36.5 us
    all_to_all x1, starting transfers between devices, per_device(): lax.all_to_all(sensitivity.reshape(cases, depth, LANES), ('x', 'core'), s...  10.4 us
    all_to_all x1, waiting for transfers between devices, per_device(): lax.all_to_all(sensitivity.reshape(cases, depth, LANES), ('x', 'core'), s...  8.13 us
    pallas_call x3, Pallas kernels, per_device(): pl.pallas_call(functools.partial(middle_kernel, element_total), out_shape...  3.6 us
  transfers between devices with their start and end apart: 1, of which 1 were waited for; matrix products, arithmetic and copies ran while one was open for 0% of the time, Pallas kernels for 0%

profile of v2, /device:TPU:1, one launch (start us, length us, event | category | flops | bytes accessed | tf_op | source)
XLA Modules:
  0.0 139.5 jit_solution(17117957892318262871)
XLA Ops:
  0.6 0.0 copy-start
  0.6 0.0 copy-start.1
  0.7 0.0 copy-start.2
  0.7 0.0 copy-start.3
  0.7 0.0 copy-start.4
  0.7 0.0 copy-start.5
  0.7 10.4 %all-to-all-start = ((f32[8,128,128]{2,1,0:T(8,128)}), f32[8,128,128]{2,1,0:T(8,128)S(1)}, u32[]{:S(2)}, u32[]{:S(2)}) async-start(f32[8,128,128]{2,1,0:T(8,128)} %bitcast.47), calls=%async_computation | async-start | bytes 1048576 | tf_op jit(solution)/shard_map/all_to_all | solution.py:281
  11.1 0.0 copy-start.6
  11.1 0.0 copy-start.7
  11.1 0.0 copy-done
  11.1 0.0 copy-done.1
  11.1 0.0 copy-done.2
  11.1 0.0 copy-done.3
  11.1 0.0 copy-done.4
  11.2 0.0 copy-done.5
  11.2 0.6 copy-done.6
  11.8 0.0 copy-done.7
  11.8 0.7 shard_map.120
  12.5 8.1 %all-to-all-done.g_ref = f32[8,128,128]{2,1,0:T(8,128)S(1)} async-done(((f32[8,128,128]{2,1,0:T(8,128)}), f32[8,128,128]{2,1,0:T(8,128)S(1)}, u32[]{:S(2)}, u32[]{:S(2)}) %all-to-all-start) | async-done | bytes 524320 | tf_op jit(solution)/shard_map/all_to_all | solution.py:281
  20.6 1.0 shard_map.121
  21.6 9.0 %all_to_all.73 = f32[16,1,128]{2,1,0:T(1,128)S(1)} all-to-all(f32[16,1,128]{2,1,0:T(1,128)S(1)} %bitcast.37), channel_id=1, replica_groups=mesh['x'=4,'core'=2,'y'=4,'z'=16] {'x','y'}, dimensions={0} | all-to-all | bytes 16384 | tf_op jit(solution)/shard_map/all_to_all | solution.py:286
  30.6 27.0 %all_to_all.74 = f32[32,1,128]{2,1,0:T(1,128)S(1)} all-to-all(f32[32,1,128]{2,1,0:T(1,128)S(1)} %broadcast_in_dim.8), channel_id=1, replica_groups=mesh['x'=4,'core'=2,'y'=4,'z'=16] {'core','z'}, dimensions={0} | all-to-all | bytes 32768 | tf_op jit(solution)/shard_map/all_to_all | solution.py:288
  57.6 1.2 shard_map.122
  58.8 9.2 %all_to_all.75 = f32[16,1,128]{2,1,0:T(1,128)S(1)} all-to-all(f32[16,1,128]{2,1,0:T(1,128)S(1)} %bitcast.38), channel_id=1, replica_groups=mesh['x'=4,'core'=2,'y'=4,'z'=16] {'x','y'}, dimensions={0} | all-to-all | bytes 16384 | tf_op jit(solution)/shard_map/all_to_all | solution.py:286
  68.1 16.5 %all_to_all.76 = f32[32,1,128]{2,1,0:T(1,128)S(1)} all-to-all(f32[32,1,128]{2,1,0:T(1,128)S(1)} %broadcast_in_dim.9), channel_id=1, replica_groups=mesh['x'=4,'core'=2,'y'=4,'z'=16] {'core','z'}, dimensions={0} | all-to-all | bytes 32768 | tf_op jit(solution)/shard_map/all_to_all | solution.py:288
  84.5 1.2 shard_map.123
  85.7 9.2 %all_to_all.77 = f32[16,1,128]{2,1,0:T(1,128)S(1)} all-to-all(f32[16,1,128]{2,1,0:T(1,128)S(1)} %bitcast.39), channel_id=1, replica_groups=mesh['x'=4,'core'=2,'y'=4,'z'=16] {'x','y'}, dimensions={0} | all-to-all | bytes 16384 | tf_op jit(solution)/shard_map/all_to_all | solution.py:286
  95.0 16.4 %all_to_all.78 = f32[32,1,128]{2,1,0:T(1,128)S(1)} all-to-all(f32[32,1,128]{2,1,0:T(1,128)S(1)} %broadcast_in_dim.10), channel_id=1, replica_groups=mesh['x'=4,'core'=2,'y'=4,'z'=16] {'core','z'}, dimensions={0} | all-to-all | bytes 32768 | tf_op jit(solution)/shard_map/all_to_all | solution.py:288
  111.4 1.2 shard_map.124
  112.6 9.2 %all_to_all.79 = f32[16,1,128]{2,1,0:T(1,128)S(1)} all-to-all(f32[16,1,128]{2,1,0:T(1,128)S(1)} %bitcast.40), channel_id=1, replica_groups=mesh['x'=4,'core'=2,'y'=4,'z'=16] {'x','y'}, dimensions={0} | all-to-all | bytes 16384 | tf_op jit(solution)/shard_map/all_to_all | solution.py:286
  121.9 16.4 %all_to_all.80 = f32[32,1,128]{2,1,0:T(1,128)S(1)} all-to-all(f32[32,1,128]{2,1,0:T(1,128)S(1)} %broadcast_in_dim.11), channel_id=1, replica_groups=mesh['x'=4,'core'=2,'y'=4,'z'=16] {'core','z'}, dimensions={0} | all-to-all | bytes 32768 | tf_op jit(solution)/shard_map/all_to_all | solution.py:288
  138.3 1.2 shard_map.125
  (8 shorter events, 0.2 us)
Async XLA Ops:
  0.6 10.5 %copy-start = (f32[1,1,16384]{2,1,0:T(1,128)S(1)}, f32[1,1,16384]{2,1,0:T(1,128)}, u32[]{:S(2)}) copy-start(f32[1,1,16384]{2,1,0:T(1,128)} %param.10) | copy-start | bytes 196612
  0.6 10.5 %copy-start.1 = (f32[1,1,16384]{2,1,0:T(1,128)S(1)}, f32[1,1,16384]{2,1,0:T(1,128)}, u32[]{:S(2)}) copy-start(f32[1,1,16384]{2,1,0:T(1,128)} %param.15) | copy-start | bytes 196612
  0.7 10.5 %copy-start.2 = (f32[1,1,16384]{2,1,0:T(1,128)S(1)}, f32[1,1,16384]{2,1,0:T(1,128)}, u32[]{:S(2)}) copy-start(f32[1,1,16384]{2,1,0:T(1,128)} %param.11) | copy-start | bytes 196612
  0.7 10.5 %copy-start.3 = (f32[1,1,16384]{2,1,0:T(1,128)S(1)}, f32[1,1,16384]{2,1,0:T(1,128)}, u32[]{:S(2)}) copy-start(f32[1,1,16384]{2,1,0:T(1,128)} %param.12) | copy-start | bytes 196612
  0.7 10.5 %copy-start.4 = (f32[1,1,16384]{2,1,0:T(1,128)S(1)}, f32[1,1,16384]{2,1,0:T(1,128)}, u32[]{:S(2)}) copy-start(f32[1,1,16384]{2,1,0:T(1,128)} %param.13) | copy-start | bytes 196612
  0.7 10.5 %copy-start.5 = (f32[1,1,16384]{2,1,0:T(1,128)S(1)}, f32[1,1,16384]{2,1,0:T(1,128)}, u32[]{:S(2)}) copy-start(f32[1,1,16384]{2,1,0:T(1,128)} %param.14) | copy-start | bytes 196612
  0.7 19.9 %all-to-all-start = ((f32[8,128,128]{2,1,0:T(8,128)}), f32[8,128,128]{2,1,0:T(8,128)S(1)}, u32[]{:S(2)}, u32[]{:S(2)}) async-start(f32[8,128,128]{2,1,0:T(8,128)} %bitcast.47), calls=%async_computation | async-start | bytes 1048576 | tf_op jit(solution)/shard_map/all_to_all | solution.py:281
  11.1 0.7 copy-start.6
  11.1 0.7 copy-start.7

commit v3 on v2

v3 whole, which is shorter than its diff:
```python
import functools

import jax
import jax.numpy as jnp
from jax import lax
from jax.experimental import pallas as pl
from jax.experimental.pallas import tpu as pltpu
from jax.sharding import Mesh
from jax.sharding import PartitionSpec as P

NEWTON = 4
PROX = 0.1
VOLFRAC = 0.4
N = 9
PAIRS = [(i, k) for i in range(N) for k in range(i + 1)]
GRAD_AT = len(PAIRS)
VOL_AT = GRAD_AT + N
LANES = 128
TARGET_AT = 16
STATE = 32
STATS = 64
CHUNK = 128
KUNROLL = 16
REPEAT_FROM = 2


def vmem():
    return pl.BlockSpec(memory_space=pltpu.VMEM)


def hbm():
    return pl.BlockSpec(memory_space=pltpu.HBM)


def total(rows):
    while rows.shape[0] > 8:
        half = rows.shape[0] // 2
        rows = rows[:half] + rows[half:]
    return jnp.sum(rows, 0, keepdims=True)


def diagonal(values, count):
    row = lax.broadcasted_iota(jnp.int32, (count, LANES), 0)
    lane = lax.broadcasted_iota(jnp.int32, (count, LANES), 1)
    return jnp.where(row == lane, values, 0.0)


def spread(gathered, table_ref):
    sums = jnp.sum(diagonal(total(gathered), table_ref.shape[0]), 1, keepdims=True)
    table_ref[...] = jnp.broadcast_to(sums, table_ref.shape)


def solve(matrix, vector):
    m = dict(matrix)
    b = list(vector)
    inverse = []
    for k in range(N):
        r = 1.0 / m[k, k]
        inverse.append(r)
        for i in range(k + 1, N):
            scaled = m[i, k] * r
            for j in range(k + 1, i + 1):
                m[i, j] = m[i, j] - scaled * m[j, k]
            b[i] = b[i] - scaled * b[k]
    x = [None] * N
    for k in reversed(range(N)):
        running = b[k]
        for i in range(k + 1, N):
            running = running - m[i, k] * x[i]
        x[k] = running * inverse[k]
    return x


def newton(table_ref, duals, targets, element_total):
    scale = 1.0 / element_total
    excess = functools.reduce(jnp.add, duals[:-1]) - 1.0
    height = jnp.maximum(excess, 0.0)
    active = jnp.where(excess > 0, 1.0, 0.0)
    matrix = {}
    for at, (i, k) in enumerate(PAIRS):
        entry = table_ref[at : at + 1, :] * scale
        if i < N - 1:
            entry = entry + active
        matrix[i, k] = entry
    trace = functools.reduce(jnp.add, [matrix[i, i] for i in range(N)])
    damping = trace * (0.5 / N) + 0.0001
    vector = []
    for i in range(N):
        matrix[i, i] = matrix[i, i] + damping
        entry = table_ref[GRAD_AT + i : GRAD_AT + i + 1, :] * scale + targets[i]
        vector.append(entry - height if i < N - 1 else entry)
    step = solve(matrix, vector)
    return [jnp.maximum(l + d, 0.1 * l) for l, d in zip(duals, step)]


def place(duals, slopes, a, b, lo, hi):
    terms = [l * g for l, g in zip(duals, slopes)]
    rise = functools.reduce(jnp.add, [jnp.maximum(m, 0.0) for m in terms])
    fall = functools.reduce(jnp.add, [jnp.minimum(m, 0.0) for m in terms])
    p = PROX + (1.001 * rise - 0.001 * fall)
    q = PROX + (0.001 * rise - 1.001 * fall)
    root_p = p * lax.rsqrt(p)
    root_q = q * lax.rsqrt(q)
    free = a * b * (root_q - root_p) / (a * root_p + b * root_q)
    return p, q, free, jnp.minimum(jnp.maximum(free, lo), hi)


def parts(g_ref, aux_ref):
    return lambda block, k, rows: g_ref[block, k, rows, :] if k < N - 1 else aux_ref[block, k - N + 1, rows, :]


def read(part, block, rows):
    held = [part(block, k, rows) for k in range(N + 4)]
    return held[:N], held[N:]


def evaluate(state_ref, part, scaled_ref, stat_ref, depth, arrive=None):
    blocks = scaled_ref.shape[1] // depth

    def fold(v):
        return jnp.sum(v.reshape(-1, 8, LANES), 0)

    def column(j, grads):
        at = pl.multiple_of(j * CHUNK, CHUNK)
        block = j // (depth // CHUNK)
        rows = pl.ds(pl.multiple_of(at - block * depth, CHUNK), CHUNK)
        if arrive is not None:
            arrive(block)
        slopes, (a, b, lo, hi) = read(part, block, rows)
        duals = [jnp.broadcast_to(state_ref[i : i + 1, :], (CHUNK, LANES)) for i in range(N)]
        p, q, free, t = place(duals, slopes, a, b, lo, hi)
        inside = (free > lo) & (free < hi)
        to_upper = a - t
        to_lower = b + t
        both = 1.0 / (to_upper * to_lower)
        ru = both * to_lower
        rl = both * to_upper
        up_at = a * ru
        down_at = b * rl
        up_two = up_at * up_at
        down_two = down_at * down_at
        curve = 2.0 * (p * up_two * ru + q * down_two * rl)
        root = jnp.where(inside, lax.rsqrt(curve), 0.0)
        cu, cd = up_two * root, down_two * root
        tu, td = t * up_at, t * down_at
        c_rise, c_fall = 1.001 * cu - 0.001 * cd, 1.001 * cd - 0.001 * cu
        t_rise, t_fall = 1.001 * tu - 0.001 * td, 1.001 * td - 0.001 * tu
        out = []
        for i, g in enumerate(slopes):
            rising = g > 0
            scaled_ref[i, pl.ds(at, CHUNK), :] = g * jnp.where(rising, c_rise, c_fall)
            out.append(grads[i] + fold(g * jnp.where(rising, t_rise, t_fall)))
        return tuple(out)

    zero = jnp.zeros((8, LANES), jnp.float32)
    steps = blocks * depth // CHUNK
    grads = lax.fori_loop(0, steps, column, (zero,) * N) if steps > 1 else column(0, (zero,) * N)
    for i in range(N):
        stat_ref[GRAD_AT + i : GRAD_AT + i + 1, :] = jnp.sum(grads[i], 0, keepdims=True)
    groups = [(0, 5), (5, 9)]
    for at, (i0, i1) in enumerate(groups):
        for k0, k1 in groups[: at + 1]:
            pairs = [(i, k) for i in range(i0, i1) for k in range(k0, min(k1, i + 1))]

            def products(j, sums, pairs=pairs):
                rows = pl.ds(pl.multiple_of(j * 8, 8), 8)
                held = {i: scaled_ref[i, rows, :] for i in sorted({i for pair in pairs for i in pair})}
                return tuple(s + held[i] * held[k] for s, (i, k) in zip(sums, pairs))

            sums = lax.fori_loop(0, blocks * depth // 8, products, (zero,) * len(pairs), unroll=KUNROLL)
            for s, pair in zip(sums, pairs):
                row = PAIRS.index(pair)
                stat_ref[row : row + 1, :] = jnp.sum(s, 0, keepdims=True)


def announce(stat_ref, message_ref):
    sums = jnp.sum(stat_ref[...], 1, keepdims=True)
    sums = total(diagonal(sums, stat_ref.shape[0]))
    message_ref[...] = jnp.broadcast_to(sums, message_ref.shape)


def prepare_kernel(
    duals_ref, case_values_ref, x_ref, x1_ref, x2_ref, gl_ref, gu_ref, w_ref,
    lower_ref, upper_ref, aux_ref, volume_ref, state_ref,
):
    x, x1, x2, w = (r[...] for r in (x_ref, x1_ref, x2_ref, w_ref))
    trend = (x - x1) * (x1 - x2)
    factor = jnp.where(trend > 0, 1.2, jnp.where(trend < 0, 0.7, 1.0))
    lower = jnp.minimum(x - factor * gl_ref[...], x - 0.01)
    upper = jnp.maximum(x + factor * gu_ref[...], x + 0.01)
    lower_ref[...] = lower
    upper_ref[...] = upper
    a = upper - x
    b = x - lower
    aux_ref[0, 0] = w
    aux_ref[0, 1] = a
    aux_ref[0, 2] = b
    aux_ref[0, 3] = jnp.maximum(jnp.maximum(lower + 0.1 * b, x - 0.2), 0.0) - x
    aux_ref[0, 4] = jnp.minimum(jnp.minimum(upper - 0.1 * a, x + 0.2), 1.0) - x
    volume_ref[...] = jnp.sum((w * x).reshape(-1, 8, LANES), 0)
    state_ref[...] = jnp.zeros(state_ref.shape, jnp.float32)
    for i in range(N):
        state_ref[i : i + 1, :] = jnp.broadcast_to(duals_ref[0:1, i : i + 1], (1, LANES))
    for i in range(N - 1):
        state_ref[TARGET_AT + i : TARGET_AT + i + 1, :] = jnp.broadcast_to(
            case_values_ref[0:1, i : i + 1], (1, LANES)
        )
    state_ref[TARGET_AT + N - 1 : TARGET_AT + N, :] = jnp.full((1, LANES), -VOLFRAC)


def first_kernel(
    g_ref, aux_ref, volume_ref, state_ref,
    message_ref, pack_ref,
    scaled_ref, stat_ref, sems,
):
    copies = [
        pltpu.make_async_copy(g_ref, pack_ref.at[:, pl.ds(0, N - 1)], sems.at[0]),
        pltpu.make_async_copy(aux_ref, pack_ref.at[:, pl.ds(N - 1, 5)], sems.at[1]),
    ]
    for copy in copies:
        copy.start()
    stat_ref[VOL_AT:, :] = jnp.zeros((STATS - VOL_AT, LANES), jnp.float32)
    stat_ref[VOL_AT : VOL_AT + 1, :] = jnp.sum(volume_ref[...], 0, keepdims=True)
    evaluate(state_ref, parts(g_ref, aux_ref), scaled_ref, stat_ref, aux_ref.shape[2])
    announce(stat_ref, message_ref)
    for copy in copies:
        copy.wait()


def update(element_total, gathered_ref, state_ref, table_ref):
    spread(gathered_ref[...], table_ref)
    duals = [state_ref[i : i + 1, :] for i in range(N)]
    targets = [state_ref[TARGET_AT + i : TARGET_AT + i + 1, :] for i in range(N)]
    targets[-1] = targets[-1] + table_ref[VOL_AT : VOL_AT + 1, :] * (1.0 / element_total)
    return newton(table_ref, duals, targets, element_total), targets


def advance(element_total, gathered_ref, state_ref, new_state_ref, stat_ref, table_ref):
    duals, targets = update(element_total, gathered_ref, state_ref, table_ref)
    new_state_ref[...] = state_ref[...]
    for i in range(N):
        new_state_ref[i : i + 1, :] = duals[i]
    new_state_ref[TARGET_AT + N - 1 : TARGET_AT + N, :] = targets[-1]
    stat_ref[VOL_AT:, :] = jnp.zeros((STATS - VOL_AT, LANES), jnp.float32)


def middle_kernel(
    element_total,
    gathered_ref, state_ref, g_ref, aux_ref,
    new_state_ref, message_ref,
    scaled_ref, stat_ref, table_ref,
):
    advance(element_total, gathered_ref, state_ref, new_state_ref, stat_ref, table_ref)
    evaluate(new_state_ref, parts(g_ref, aux_ref), scaled_ref, stat_ref, aux_ref.shape[2])
    announce(stat_ref, message_ref)


def repeated_kernel(
    element_total,
    gathered_ref, state_ref, pack_ref,
    new_state_ref, message_ref,
    scaled_ref, stat_ref, table_ref, held_ref, sems,
):
    def copy(block):
        return pltpu.make_async_copy(pack_ref.at[block], held_ref.at[block], sems.at[block])

    for block in range(held_ref.shape[0]):
        copy(block).start()
    advance(element_total, gathered_ref, state_ref, new_state_ref, stat_ref, table_ref)

    def part(block, k, rows):
        return held_ref[block, k, rows, :]

    evaluate(new_state_ref, part, scaled_ref, stat_ref, held_ref.shape[2], lambda block: copy(block).wait())
    announce(stat_ref, message_ref)


def last_kernel(
    element_total,
    gathered_ref, state_ref, g_ref, aux_ref, x_ref,
    design_ref, duals_ref,
    table_ref,
):
    duals, _ = update(element_total, gathered_ref, state_ref, table_ref)
    lane = lax.broadcasted_iota(jnp.int32, (1, LANES), 1)
    row = jnp.zeros((1, LANES), jnp.float32)
    for i in range(N):
        row = jnp.where(lane == i, duals[i], row)
    duals_ref[...] = row[:, : duals_ref.shape[1]]
    depth = x_ref.shape[0]
    wide = [jnp.broadcast_to(l, (depth, LANES)) for l in duals]
    slopes, (a, b, lo, hi) = read(parts(g_ref, aux_ref), 0, pl.ds(0, depth))
    _, _, _, t = place(wide, slopes, a, b, lo, hi)
    design_ref[...] = x_ref[...] + t


def f32(*shape):
    return jax.ShapeDtypeStruct(shape, jnp.float32)


PARAMS = pltpu.CompilerParams(vmem_limit_bytes=16 * 1024 * 1024)
WIDE_PARAMS = pltpu.CompilerParams(vmem_limit_bytes=52 * 1024 * 1024)
NEAR = ("x", "y")
FAR = ("core", "z")
REST = ("x", "core", "z")
REPEATED = ("y",)


def scratch(blocks, depth):
    return [
        pltpu.VMEM((N, blocks * depth, LANES), jnp.float32),
        pltpu.VMEM((STATS, LANES), jnp.float32),
        pltpu.VMEM((STATS, LANES), jnp.float32),
    ]


def per_device(sensitivity, x, x1, x2, gl, gu, w, case_values, duals_start):
    sizes = {name: lax.axis_size(name) for name in ("x", "core", "y", "z")}
    near = sizes["x"] * sizes["y"]
    far = sizes["core"] * sizes["z"]
    rest = sizes["x"] * far
    cases = sizes["x"] * sizes["core"]
    depth = x.size // LANES
    element_total = float(x.size * near * far)
    shape = x.shape
    x, x1, x2, gl, gu, w = (v.reshape(depth, LANES) for v in (x, x1, x2, gl, gu, w))
    g = lax.all_to_all(
        sensitivity.reshape(cases, depth, LANES), ("x", "core"), split_axis=0, concat_axis=0, tiled=True
    ).reshape(1, cases, depth, LANES)

    def exchange(message, axes):
        return lax.all_to_all(message, axes, split_axis=0, concat_axis=0, tiled=True)

    def gather(message):
        if message.shape[0] == rest:
            return exchange(message, REST)
        part = jnp.sum(exchange(message, NEAR), 0, keepdims=True)
        return exchange(jnp.broadcast_to(part, (far, LANES)), FAR)

    lower, upper, aux, volume, state = pl.pallas_call(
        prepare_kernel,
        out_shape=(
            f32(depth, LANES), f32(depth, LANES), f32(1, 5, depth, LANES), f32(8, LANES), f32(STATE, LANES),
        ),
        in_specs=[vmem()] * 8,
        out_specs=(vmem(),) * 5,
        compiler_params=PARAMS,
        cost_estimate=pl.CostEstimate(flops=10_000_000_000, bytes_accessed=40_000_000, transcendentals=0),
    )(duals_start.reshape(1, -1), case_values.reshape(1, -1), x, x1, x2, gl, gu, w)
    message, pack = pl.pallas_call(
        first_kernel,
        out_shape=(f32(near, LANES), f32(1, N + 4, depth, LANES)),
        in_specs=[vmem()] * 4,
        out_specs=(vmem(), hbm()),
        scratch_shapes=scratch(1, depth)[:2] + [pltpu.SemaphoreType.DMA((2,))],
        compiler_params=PARAMS,
    )(g, aux, volume, state)
    pack = lax.all_gather(pack, REPEATED, tiled=True)
    blocks = pack.shape[0]
    for step in range(1, NEWTON):
        if step < REPEAT_FROM:
            state, message = pl.pallas_call(
                functools.partial(middle_kernel, element_total),
                out_shape=(f32(STATE, LANES), f32(near, LANES)),
                in_specs=[vmem()] * 4,
                out_specs=(vmem(),) * 2,
                scratch_shapes=scratch(1, depth),
                compiler_params=PARAMS,
            )(gather(message), state, g, aux)
        else:
            state, message = pl.pallas_call(
                functools.partial(repeated_kernel, element_total),
                out_shape=(f32(STATE, LANES), f32(rest, LANES)),
                in_specs=[vmem()] * 2 + [hbm()],
                out_specs=(vmem(),) * 2,
                scratch_shapes=scratch(blocks, depth)
                + [pltpu.VMEM(pack.shape, jnp.float32), pltpu.SemaphoreType.DMA((blocks,))],
                compiler_params=WIDE_PARAMS,
            )(gather(message), state, pack)
    design, duals = pl.pallas_call(
        functools.partial(last_kernel, element_total),
        out_shape=(f32(depth, LANES), f32(1, N)),
        in_specs=[vmem()] * 5,
        out_specs=(vmem(),) * 2,
        scratch_shapes=scratch(1, depth)[2:],
        compiler_params=PARAMS,
    )(gather(message), state, g, aux, x)
    return design.reshape(shape), lower.reshape(shape), upper.reshape(shape), duals.reshape(N)


def solution(mesh):
    cases, slabs = mesh.devices.shape
    fine = Mesh(mesh.devices.reshape(cases // 2, 2, 4, slabs // 4), ("x", "core", "y", "z"))
    case, slab = ("x", "core"), ("y", "z")
    design = P(slab, case, None)
    return jax.shard_map(
        per_device,
        mesh=fine,
        in_specs=(P(case, slab),) + (design,) * 6 + (P(), P()),
        out_specs=(design, design, design, P()),
        check_vma=False,
    )
```

time: 140 us -> 147 us (1.050)
  between operations: 0.74 us -> 14.1 us
  blocking collectives: 113 us -> 103 us
  local copies, waits for them, and re-layouts: 0.69 us -> 6.37 us
  waiting for transfers between devices: 8.13 us -> 2.46 us
  Pallas kernels: 6.47 us -> 10.8 us
    all_to_all x8 -> x6, blocking collectives: 113 us -> 103 us  [exchange(): lax.all_to_all(message, axes, split_axis=0, concat_axis=0, tiled=True)]
    pallas_call x1 -> x3, Pallas kernels: 1 us -> 8.12 us  [the longest x2 7.19 us: per_device(): pl.pallas_call(functools.partial(repeated_kernel, element_total), out_sha...]
    unnamed x16 -> x18, local copies, waits for them, and re-layouts: 0.64 us -> 6.35 us
    all_to_all x1, waiting for transfers between devices: 8.13 us -> 2.44 us  [per_device(): lax.all_to_all(sensitivity.reshape(cases, depth, LANES), ('x', 'core'), s...]
    pallas_call x3 -> x1, Pallas kernels: 3.6 us -> 0.97 us  [per_device(): pl.pallas_call(functools.partial(middle_kernel, element_total), out_shape...]
  transfers between devices with their start and end apart: 1 -> 2, of which waited for: 1 -> 1; matrix products, arithmetic and copies ran while one was open for 0% -> 0% of each run, Pallas kernels for 0% -> 1%
where the time goes in v3:
time: 147 us
  blocking collectives  103 us (70%)
  between operations  14.1 us (10%)
  Pallas kernels  10.8 us (7%)
  starting transfers between devices  10.3 us (7%)
  local copies, waits for them, and re-layouts  6.37 us (4%)
  waiting for transfers between devices  2.46 us (2%)
    all_to_all x6, blocking collectives, exchange(): lax.all_to_all(message, axes, split_axis=0, concat_axis=0, tiled=True)  103 us
    all_to_all x1, starting transfers between devices, per_device(): lax.all_to_all(sensitivity.reshape(cases, depth, LANES), ('x', 'core'), s...  10.3 us
    pallas_call x2, Pallas kernels, per_device(): pl.pallas_call(functools.partial(repeated_kernel, element_total), out_sha...  7.19 us
    unnamed x18, local copies, waits for them, and re-layouts  6.35 us
  transfers between devices with their start and end apart: 2, of which 1 were waited for; matrix products, arithmetic and copies ran while one was open for 0% of the time, Pallas kernels for 1%

profile of v3, /device:TPU:1, one launch (start us, length us, event | category | flops | bytes accessed | tf_op | source)
XLA Modules:
  0.0 146.7 jit_solution(837814345984545786)
XLA Ops:
  7.2 10.3 %all-to-all-start = ((f32[8,128,128]{2,1,0:T(8,128)}), f32[8,128,128]{2,1,0:T(8,128)S(1)}, u32[]{:S(2)}, u32[]{:S(2)}) async-start(f32[8,128,128]{2,1,0:T(8,128)} %bitcast.50), calls=%async_computation | async-start | bytes 1048576 | tf_op jit(solution)/shard_map/all_to_all | solution.py:327
  17.4 0.0 all-gather.2.cloned.1.call-start
  17.5 0.0 copy-start
  17.5 0.8 copy-done
  18.3 0.0 copy-start.2
  18.3 0.8 copy-done.2
  19.1 0.0 copy-start.3
  19.1 0.8 copy-done.3
  20.0 0.0 copy-start.4
  20.0 0.8 copy-done.4
  20.8 0.0 copy-start.5
  20.8 0.8 copy-done.5
  21.7 0.0 copy-start.6
  21.7 0.8 copy-done.6
  22.5 0.0 copy-start.7
  22.5 0.7 copy-done.7
  23.1 0.7 copy-done.8
  23.8 0.7 shard_map.120
  24.5 2.4 %all-to-all-done = f32[8,128,128]{2,1,0:T(8,128)S(1)} async-done(((f32[8,128,128]{2,1,0:T(8,128)}), f32[8,128,128]{2,1,0:T(8,128)S(1)}, u32[]{:S(2)}, u32[]{:S(2)}) %all-to-all-start) | async-done | bytes 524320 | tf_op jit(solution)/shard_map/all_to_all | solution.py:327
  26.9 0.9 shard_map.121
  27.9 0.0 all-gather.2.cloned.1.call-update
  27.9 9.0 %all_to_all.61 = f32[16,1,128]{2,1,0:T(1,128)S(1)} all-to-all(f32[16,1,128]{2,1,0:T(1,128)S(1)} %bitcast.41), channel_id=1, replica_groups=mesh['x'=4,'core'=2,'y'=4,'z'=16] {'x','y'}, dimensions={0} | all-to-all | bytes 16384 | tf_op jit(solution)/shard_map/all_to_all | solution.py:332
  36.9 27.0 %all_to_all.62 = f32[32,1,128]{2,1,0:T(1,128)S(1)} all-to-all(f32[32,1,128]{2,1,0:T(1,128)S(1)} %broadcast_in_dim.4), channel_id=1, replica_groups=mesh['x'=4,'core'=2,'y'=4,'z'=16] {'core','z'}, dimensions={0} | all-to-all | bytes 32768 | tf_op jit(solution)/shard_map/all_to_all | solution.py:332
  63.9 1.0 shard_map.122
  64.9 9.1 %all_to_all.63 = f32[16,1,128]{2,1,0:T(1,128)S(1)} all-to-all(f32[16,1,128]{2,1,0:T(1,128)S(1)} %bitcast.42), channel_id=1, replica_groups=mesh['x'=4,'core'=2,'y'=4,'z'=16] {'x','y'}, dimensions={0} | all-to-all | bytes 16384 | tf_op jit(solution)/shard_map/all_to_all | solution.py:332
  74.0 16.5 %all_to_all.64 = f32[32,1,128]{2,1,0:T(1,128)S(1)} all-to-all(f32[32,1,128]{2,1,0:T(1,128)S(1)} %broadcast_in_dim.5), channel_id=1, replica_groups=mesh['x'=4,'core'=2,'y'=4,'z'=16] {'core','z'}, dimensions={0} | all-to-all | bytes 32768 | tf_op jit(solution)/shard_map/all_to_all | solution.py:332
  90.5 3.6 %shard_map.123 = (f32[32,128]{1,0:T(8,128)S(1)}, f32[128,128]{1,0:T(8,128)S(1)}) custom-call(f32[32,128]{1,0:T(8,128)S(1)} %bitcast.35, f32[32,128]{1,0:T(8,128)S(1)} %get-tuple-element.24.state_ref, f32[4,13,128,128]{3,2,1,0:T(8,128)} %all-gather.2.cloned.1.call-done.pack_ref), custom_call_target="tpu_custom_call" | custom-call | tf_op jit(solution)/shard_map/pallas_call | solution.py:371
  94.2 20.6 %all_to_all.65 = f32[128,1,128]{2,1,0:T(1,128)S(1)} all-to-all(f32[128,1,128]{2,1,0:T(1,128)S(1)} %bitcast.38), channel_id=1, replica_groups=mesh['x'=4,'core'=2,'y'=4,'z'=16] {'x','core','z'}, dimensions={0} | all-to-all | bytes 131072 | tf_op jit(solution)/shard_map/all_to_all | solution.py:332
  114.8 3.6 %shard_map.124 = (f32[32,128]{1,0:T(8,128)S(1)}, f32[128,128]{1,0:T(8,128)S(1)}) custom-call(f32[128,128]{1,0:T(8,128)S(1)} %bitcast.33, f32[32,128]{1,0:T(8,128)S(1)} %get-tuple-element.27.state_ref, f32[4,13,128,128]{3,2,1,0:T(8,128)} %all-gather.2.cloned.1.call-done.pack_ref), custom_call_target="tpu_custom_call" | custom-call | tf_op jit(solution)/shard_map/pallas_call | solution.py:371
  118.4 20.5 %all_to_all.66 = f32[128,1,128]{2,1,0:T(1,128)S(1)} all-to-all(f32[128,1,128]{2,1,0:T(1,128)S(1)} %bitcast.37), channel_id=1, replica_groups=mesh['x'=4,'core'=2,'y'=4,'z'=16] {'x','core','z'}, dimensions={0} | all-to-all | bytes 131072 | tf_op jit(solution)/shard_map/all_to_all | solution.py:332
  138.9 0.0 copy-done.1
  138.9 1.0 shard_map.125
  (7 shorter events, 0.1 us)
Async XLA Ops:
  7.2 19.8 %all-to-all-start = ((f32[8,128,128]{2,1,0:T(8,128)}), f32[8,128,128]{2,1,0:T(8,128)S(1)}, u32[]{:S(2)}, u32[]{:S(2)}) async-start(f32[8,128,128]{2,1,0:T(8,128)} %bitcast.50), calls=%async_computation | async-start | bytes 1048576 | tf_op jit(solution)/shard_map/all_to_all | solution.py:327
  17.4 73.1 %all-gather.2.cloned.1.call-start = ((), (), s32[]{:S(2)}) async-start(), calls=%async_computation.7 | async-start | bytes 4259840 | tf_op jit(solution)/shard_map/all_gather | solution.py:358
  17.5 0.8 copy-start
  18.3 0.8 copy-start.2
  19.1 0.8 copy-start.3
  20.0 0.8 copy-start.4
  20.8 0.8 copy-start.5
  21.7 0.8 copy-start.6
  22.5 0.7 copy-start.7
  23.1 0.7 copy-start.8
  90.5 48.3 %copy-start.1 = (f32[1,1,16384]{2,1,0:T(1,128)S(1)}, f32[1,1,16384]{2,1,0:T(1,128)}, u32[]{:S(2)}) copy-start(f32[1,1,16384]{2,1,0:T(1,128)} %param.10) | copy-start | bytes 196612
Sparse Core Ops, SparseCore 0:
  28.0 47.8 all-gather.1

commit v4 on v3

--- a/solution.py
+++ b/solution.py
@@ -21,15 +21,10 @@
 STATS = 64
 CHUNK = 128
 KUNROLL = 16
-REPEAT_FROM = 2
 
 
 def vmem():
     return pl.BlockSpec(memory_space=pltpu.VMEM)
-
-
-def hbm():
-    return pl.BlockSpec(memory_space=pltpu.HBM)
 
 
 def total(rows):
@@ -114,7 +109,7 @@
     return held[:N], held[N:]
 
 
-def evaluate(state_ref, part, scaled_ref, stat_ref, depth, arrive=None):
+def evaluate(state_ref, part, scaled_ref, stat_ref, depth):
     blocks = scaled_ref.shape[1] // depth
 
     def fold(v):
@@ -124,8 +119,6 @@
         at = pl.multiple_of(j * CHUNK, CHUNK)
         block = j // (depth // CHUNK)
         rows = pl.ds(pl.multiple_of(at - block * depth, CHUNK), CHUNK)
-        if arrive is not None:
-            arrive(block)
         slopes, (a, b, lo, hi) = read(part, block, rows)
         duals = [jnp.broadcast_to(state_ref[i : i + 1, :], (CHUNK, LANES)) for i in range(N)]
         p, q, free, t = place(duals, slopes, a, b, lo, hi)
@@ -208,23 +201,11 @@
     state_ref[TARGET_AT + N - 1 : TARGET_AT + N, :] = jnp.full((1, LANES), -VOLFRAC)
 
 
-def first_kernel(
-    g_ref, aux_ref, volume_ref, state_ref,
-    message_ref, pack_ref,
-    scaled_ref, stat_ref, sems,
-):
-    copies = [
-        pltpu.make_async_copy(g_ref, pack_ref.at[:, pl.ds(0, N - 1)], sems.at[0]),
-        pltpu.make_async_copy(aux_ref, pack_ref.at[:, pl.ds(N - 1, 5)], sems.at[1]),
-    ]
-    for copy in copies:
-        copy.start()
+def first_kernel(g_ref, aux_ref, volume_ref, state_ref, message_ref, scaled_ref, stat_ref):
     stat_ref[VOL_AT:, :] = jnp.zeros((STATS - VOL_AT, LANES), jnp.float32)
     stat_ref[VOL_AT : VOL_AT + 1, :] = jnp.sum(volume_ref[...], 0, keepdims=True)
     evaluate(state_ref, parts(g_ref, aux_ref), scaled_ref, stat_ref, aux_ref.shape[2])
     announce(stat_ref, message_ref)
-    for copy in copies:
-        copy.wait()
 
 
 def update(element_total, gathered_ref, state_ref, table_ref):
@@ -255,26 +236,6 @@
     announce(stat_ref, message_ref)
 
 
-def repeated_kernel(
-    element_total,
-    gathered_ref, state_ref, pack_ref,
-    new_state_ref, message_ref,
-    scaled_ref, stat_ref, table_ref, held_ref, sems,
-):
-    def copy(block):
-        return pltpu.make_async_copy(pack_ref.at[block], held_ref.at[block], sems.at[block])
-
-    for block in range(held_ref.shape[0]):
-        copy(block).start()
-    advance(element_total, gathered_ref, state_ref, new_state_ref, stat_ref, table_ref)
-
-    def part(block, k, rows):
-        return held_ref[block, k, rows, :]
-
-    evaluate(new_state_ref, part, scaled_ref, stat_ref, held_ref.shape[2], lambda block: copy(block).wait())
-    announce(stat_ref, message_ref)
-
-
 def last_kernel(
     element_total,
     gathered_ref, state_ref, g_ref, aux_ref, x_ref,
@@ -299,11 +260,8 @@
 
 
 PARAMS = pltpu.CompilerParams(vmem_limit_bytes=16 * 1024 * 1024)
-WIDE_PARAMS = pltpu.CompilerParams(vmem_limit_bytes=52 * 1024 * 1024)
 NEAR = ("x", "y")
 FAR = ("core", "z")
-REST = ("x", "core", "z")
-REPEATED = ("y",)
 
 
 def scratch(blocks, depth):
@@ -318,7 +276,6 @@
     sizes = {name: lax.axis_size(name) for name in ("x", "core", "y", "z")}
     near = sizes["x"] * sizes["y"]
     far = sizes["core"] * sizes["z"]
-    rest = sizes["x"] * far
     cases = sizes["x"] * sizes["core"]
     depth = x.size // LANES
     element_total = float(x.size * near * far)
@@ -332,8 +289,6 @@
         return lax.all_to_all(message, axes, split_axis=0, concat_axis=0, tiled=True)
 
     def gather(message):
-        if message.shape[0] == rest:
-            return exchange(message, REST)
         part = jnp.sum(exchange(message, NEAR), 0, keepdims=True)
         return exchange(jnp.broadcast_to(part, (far, LANES)), FAR)
 
@@ -347,36 +302,23 @@
         compiler_params=PARAMS,
         cost_estimate=pl.CostEstimate(flops=10_000_000_000, bytes_accessed=40_000_000, transcendentals=0),
     )(duals_start.reshape(1, -1), case_values.reshape(1, -1), x, x1, x2, gl, gu, w)
-    message, pack = pl.pallas_call(
+    message = pl.pallas_call(
         first_kernel,
-        out_shape=(f32(near, LANES), f32(1, N + 4, depth, LANES)),
+        out_shape=f32(near, LANES),
         in_specs=[vmem()] * 4,
-        out_specs=(vmem(), hbm()),
-        scratch_shapes=scratch(1, depth)[:2] + [pltpu.SemaphoreType.DMA((2,))],
+        out_specs=vmem(),
+        scratch_shapes=scratch(1, depth)[:2],
         compiler_params=PARAMS,
     )(g, aux, volume, state)
-    pack = lax.all_gather(pack, REPEATED, tiled=True)
-    blocks = pack.shape[0]
-    for step in range(1, NEWTON):
-        if step < REPEAT_FROM:
-            state, message = pl.pallas_call(
-                functools.partial(middle_kernel, element_total),
-                out_shape=(f32(STATE, LANES), f32(near, LANES)),
-                in_specs=[vmem()] * 4,
-                out_specs=(vmem(),) * 2,
-                scratch_shapes=scratch(1, depth),
-                compiler_params=PARAMS,
-            )(gather(message), state, g, aux)
-        else:
-            state, message = pl.pallas_call(
-                functools.partial(repeated_kernel, element_total),
-                out_shape=(f32(STATE, LANES), f32(rest, LANES)),
-                in_specs=[vmem()] * 2 + [hbm()],
-                out_specs=(vmem(),) * 2,
-                scratch_shapes=scratch(blocks, depth)
-                + [pltpu.VMEM(pack.shape, jnp.float32), pltpu.SemaphoreType.DMA((blocks,))],
-                compiler_params=WIDE_PARAMS,
-            )(gather(message), state, pack)
+    for _ in range(NEWTON - 1):
+        state, message = pl.pallas_call(
+            functools.partial(middle_kernel, element_total),
+            out_shape=(f32(STATE, LANES), f32(near, LANES)),
+            in_specs=[vmem()] * 4,
+            out_specs=(vmem(),) * 2,
+            scratch_shapes=scratch(1, depth),
+            compiler_params=PARAMS,
+        )(gather(message), state, g, aux)
     design, duals = pl.pallas_call(
         functools.partial(last_kernel, element_total),
         out_shape=(f32(depth, LANES), f32(1, N)),

time: 147 us -> 139 us (0.946)
  between operations: 14.1 us -> 0.74 us
  blocking collectives: 103 us -> 113 us
  local copies, waits for them, and re-layouts: 6.37 us -> 0.69 us
  waiting for transfers between devices: 2.46 us -> 8.12 us
  Pallas kernels: 10.8 us -> 5.4 us
    all_to_all x6 -> x8, blocking collectives: 103 us -> 113 us  [exchange(): lax.all_to_all(message, axes, split_axis=0, concat_axis=0, tiled=True)]
    pallas_call x3 -> x1, Pallas kernels: 8.12 us -> 0.76 us  [per_device(): pl.pallas_call(first_kernel, out_shape=f32(near, LANES), in_specs=[vmem()...]
    unnamed x18 -> x16, local copies, waits for them, and re-layouts: 6.35 us -> 0.64 us
    all_to_all x1, waiting for transfers between devices: 2.44 us -> 8.12 us  [per_device(): lax.all_to_all(sensitivity.reshape(cases, depth, LANES), ('x', 'core'), s...]
    pallas_call x1 -> x3, Pallas kernels: 0.97 us -> 2.91 us  [per_device(): pl.pallas_call(functools.partial(middle_kernel, element_total), out_shape...]
  transfers between devices with their start and end apart: 2 -> 1, of which waited for: 1 -> 1; matrix products, arithmetic and copies ran while one was open for 0% -> 0% of each run, Pallas kernels for 1% -> 1%
where the time goes in v4:
time: 139 us; the launch traced here: 138 us
  blocking collectives  113 us (81%)
  starting transfers between devices  10.4 us (7%)
  waiting for transfers between devices  8.12 us (6%)
  Pallas kernels  5.4 us (4%)
    all_to_all x8, blocking collectives, exchange(): lax.all_to_all(message, axes, split_axis=0, concat_axis=0, tiled=True)  113 us
    all_to_all x1, starting transfers between devices, per_device(): lax.all_to_all(sensitivity.reshape(cases, depth, LANES), ('x', 'core'), s...  10.4 us
    all_to_all x1, waiting for transfers between devices, per_device(): lax.all_to_all(sensitivity.reshape(cases, depth, LANES), ('x', 'core'), s...  8.12 us
    pallas_call x3, Pallas kernels, per_device(): pl.pallas_call(functools.partial(middle_kernel, element_total), out_shape...  2.91 us
  transfers between devices with their start and end apart: 1, of which 1 were waited for; matrix products, arithmetic and copies ran while one was open for 0% of the time, Pallas kernels for 1%

profile of v4, /device:TPU:1, one launch (start us, length us, event | category | flops | bytes accessed | tf_op | source)
XLA Modules:
  0.0 138.2 jit_solution(8700657176849519084)
XLA Ops:
  0.6 0.0 copy-start
  0.6 0.0 copy-start.1
  0.7 0.0 copy-start.2
  0.7 0.0 copy-start.3
  0.7 0.0 copy-start.4
  0.7 0.0 copy-start.5
  0.7 10.4 %all-to-all-start = ((f32[8,128,128]{2,1,0:T(8,128)}), f32[8,128,128]{2,1,0:T(8,128)S(1)}, u32[]{:S(2)}, u32[]{:S(2)}) async-start(f32[8,128,128]{2,1,0:T(8,128)} %bitcast.52), calls=%async_computation | async-start | bytes 1048576 | tf_op jit(solution)/shard_map/all_to_all | solution.py:284
  11.1 0.0 copy-start.6
  11.1 0.0 copy-start.7
  11.1 0.0 copy-done
  11.1 0.0 copy-done.1
  11.1 0.0 copy-done.2
  11.1 0.0 copy-done.3
  11.1 0.0 copy-done.4
  11.2 0.0 copy-done.5
  11.2 0.6 copy-done.6
  11.8 0.0 copy-done.7
  11.8 0.7 shard_map.120
  12.5 8.1 %all-to-all-done = f32[8,128,128]{2,1,0:T(8,128)S(1)} async-done(((f32[8,128,128]{2,1,0:T(8,128)}), f32[8,128,128]{2,1,0:T(8,128)S(1)}, u32[]{:S(2)}, u32[]{:S(2)}) %all-to-all-start) | async-done | bytes 524320 | tf_op jit(solution)/shard_map/all_to_all | solution.py:284
  20.6 0.8 shard_map.121
  21.4 8.9 %all_to_all.73 = f32[16,1,128]{2,1,0:T(1,128)S(1)} all-to-all(f32[16,1,128]{2,1,0:T(1,128)S(1)} %bitcast.41), channel_id=1, replica_groups=mesh['x'=4,'core'=2,'y'=4,'z'=16] {'x','y'}, dimensions={0} | all-to-all | bytes 16384 | tf_op jit(solution)/shard_map/all_to_all | solution.py:289
  30.4 27.0 %all_to_all.74 = f32[32,1,128]{2,1,0:T(1,128)S(1)} all-to-all(f32[32,1,128]{2,1,0:T(1,128)S(1)} %broadcast_in_dim.8), channel_id=1, replica_groups=mesh['x'=4,'core'=2,'y'=4,'z'=16] {'core','z'}, dimensions={0} | all-to-all | bytes 32768 | tf_op jit(solution)/shard_map/all_to_all | solution.py:289
  57.3 1.0 shard_map.122
  58.3 9.1 %all_to_all.75 = f32[16,1,128]{2,1,0:T(1,128)S(1)} all-to-all(f32[16,1,128]{2,1,0:T(1,128)S(1)} %bitcast.42), channel_id=1, replica_groups=mesh['x'=4,'core'=2,'y'=4,'z'=16] {'x','y'}, dimensions={0} | all-to-all | bytes 16384 | tf_op jit(solution)/shard_map/all_to_all | solution.py:289
  67.5 16.5 %all_to_all.76 = f32[32,1,128]{2,1,0:T(1,128)S(1)} all-to-all(f32[32,1,128]{2,1,0:T(1,128)S(1)} %broadcast_in_dim.9), channel_id=1, replica_groups=mesh['x'=4,'core'=2,'y'=4,'z'=16] {'core','z'}, dimensions={0} | all-to-all | bytes 32768 | tf_op jit(solution)/shard_map/all_to_all | solution.py:289
  84.0 1.0 shard_map.123
  84.9 9.1 %all_to_all.77 = f32[16,1,128]{2,1,0:T(1,128)S(1)} all-to-all(f32[16,1,128]{2,1,0:T(1,128)S(1)} %bitcast.43), channel_id=1, replica_groups=mesh['x'=4,'core'=2,'y'=4,'z'=16] {'x','y'}, dimensions={0} | all-to-all | bytes 16384 | tf_op jit(solution)/shard_map/all_to_all | solution.py:289
  94.1 16.4 %all_to_all.78 = f32[32,1,128]{2,1,0:T(1,128)S(1)} all-to-all(f32[32,1,128]{2,1,0:T(1,128)S(1)} %broadcast_in_dim.10), channel_id=1, replica_groups=mesh['x'=4,'core'=2,'y'=4,'z'=16] {'core','z'}, dimensions={0} | all-to-all | bytes 32768 | tf_op jit(solution)/shard_map/all_to_all | solution.py:289
  110.6 1.0 shard_map.124
  111.5 9.1 %all_to_all.79 = f32[16,1,128]{2,1,0:T(1,128)S(1)} all-to-all(f32[16,1,128]{2,1,0:T(1,128)S(1)} %bitcast.44), channel_id=1, replica_groups=mesh['x'=4,'core'=2,'y'=4,'z'=16] {'x','y'}, dimensions={0} | all-to-all | bytes 16384 | tf_op jit(solution)/shard_map/all_to_all | solution.py:289
  120.7 16.4 %all_to_all.80 = f32[32,1,128]{2,1,0:T(1,128)S(1)} all-to-all(f32[32,1,128]{2,1,0:T(1,128)S(1)} %broadcast_in_dim.11), channel_id=1, replica_groups=mesh['x'=4,'core'=2,'y'=4,'z'=16] {'core','z'}, dimensions={0} | all-to-all | bytes 32768 | tf_op jit(solution)/shard_map/all_to_all | solution.py:289
  137.1 1.0 shard_map.125
  (8 shorter events, 0.2 us)
Async XLA Ops:
  0.6 10.5 %copy-start = (f32[1,1,16384]{2,1,0:T(1,128)S(1)}, f32[1,1,16384]{2,1,0:T(1,128)}, u32[]{:S(2)}) copy-start(f32[1,1,16384]{2,1,0:T(1,128)} %param.10) | copy-start | bytes 196612
  0.6 10.5 %copy-start.1 = (f32[1,1,16384]{2,1,0:T(1,128)S(1)}, f32[1,1,16384]{2,1,0:T(1,128)}, u32[]{:S(2)}) copy-start(f32[1,1,16384]{2,1,0:T(1,128)} %param.11) | copy-start | bytes 196612
  0.7 10.5 %copy-start.2 = (f32[1,1,16384]{2,1,0:T(1,128)S(1)}, f32[1,1,16384]{2,1,0:T(1,128)}, u32[]{:S(2)}) copy-start(f32[1,1,16384]{2,1,0:T(1,128)} %param.12) | copy-start | bytes 196612
  0.7 10.5 %copy-start.3 = (f32[1,1,16384]{2,1,0:T(1,128)S(1)}, f32[1,1,16384]{2,1,0:T(1,128)}, u32[]{:S(2)}) copy-start(f32[1,1,16384]{2,1,0:T(1,128)} %param.13) | copy-start | bytes 196612
  0.7 10.5 %copy-start.4 = (f32[1,1,16384]{2,1,0:T(1,128)S(1)}, f32[1,1,16384]{2,1,0:T(1,128)}, u32[]{:S(2)}) copy-start(f32[1,1,16384]{2,1,0:T(1,128)} %param.14) | copy-start | bytes 196612
  0.7 10.5 %copy-start.5 = (f32[1,1,16384]{2,1,0:T(1,128)S(1)}, f32[1,1,16384]{2,1,0:T(1,128)}, u32[]{:S(2)}) copy-start(f32[1,1,16384]{2,1,0:T(1,128)} %param.15) | copy-start | bytes 196612
  0.7 19.9 %all-to-all-start = ((f32[8,128,128]{2,1,0:T(8,128)}), f32[8,128,128]{2,1,0:T(8,128)S(1)}, u32[]{:S(2)}, u32[]{:S(2)}) async-start(f32[8,128,128]{2,1,0:T(8,128)} %bitcast.52), calls=%async_computation | async-start | bytes 1048576 | tf_op jit(solution)/shard_map/all_to_all | solution.py:284
  11.1 0.7 copy-start.6
  11.1 0.7 copy-start.7

commit v5 on v4

--- a/solution.py
+++ b/solution.py
@@ -21,6 +21,7 @@
 STATS = 64
 CHUNK = 128
 KUNROLL = 16
+ORDER = ("nf", "nf", "nf", "fn")
 
 
 def vmem():
@@ -288,9 +289,12 @@
     def exchange(message, axes):
         return lax.all_to_all(message, axes, split_axis=0, concat_axis=0, tiled=True)
 
-    def gather(message):
-        part = jnp.sum(exchange(message, NEAR), 0, keepdims=True)
-        return exchange(jnp.broadcast_to(part, (far, LANES)), FAR)
+    stages = {"n": (NEAR, near), "f": (FAR, far)}
+
+    def gather(message, order):
+        (first, _), (second, count) = (stages[name] for name in order)
+        part = jnp.sum(exchange(message, first), 0, keepdims=True)
+        return exchange(jnp.broadcast_to(part, (count, LANES)), second)
 
     lower, upper, aux, volume, state = pl.pallas_call(
         prepare_kernel,
@@ -304,21 +308,21 @@
     )(duals_start.reshape(1, -1), case_values.reshape(1, -1), x, x1, x2, gl, gu, w)
     message = pl.pallas_call(
         first_kernel,
-        out_shape=f32(near, LANES),
+        out_shape=f32(stages[ORDER[0][0]][1], LANES),
         in_specs=[vmem()] * 4,
         out_specs=vmem(),
         scratch_shapes=scratch(1, depth)[:2],
         compiler_params=PARAMS,
     )(g, aux, volume, state)
-    for _ in range(NEWTON - 1):
+    for step in range(1, NEWTON):
         state, message = pl.pallas_call(
             functools.partial(middle_kernel, element_total),
-            out_shape=(f32(STATE, LANES), f32(near, LANES)),
+            out_shape=(f32(STATE, LANES), f32(stages[ORDER[step][0]][1], LANES)),
             in_specs=[vmem()] * 4,
             out_specs=(vmem(),) * 2,
             scratch_shapes=scratch(1, depth),
             compiler_params=PARAMS,
-        )(gather(message), state, g, aux)
+        )(gather(message, ORDER[step - 1]), state, g, aux)
     design, duals = pl.pallas_call(
         functools.partial(last_kernel, element_total),
         out_shape=(f32(depth, LANES), f32(1, N)),
@@ -326,7 +330,7 @@
         out_specs=(vmem(),) * 2,
         scratch_shapes=scratch(1, depth)[2:],
         compiler_params=PARAMS,
-    )(gather(message), state, g, aux, x)
+    )(gather(message, ORDER[-1]), state, g, aux, x)
     return design.reshape(shape), lower.reshape(shape), upper.reshape(shape), duals.reshape(N)
 
 

time: 139 us -> 137 us (0.986)
  blocking collectives: 113 us -> 111 us
    all_to_all x8, blocking collectives: 113 us -> 111 us  [exchange(): lax.all_to_all(message, axes, split_axis=0, concat_axis=0, tiled=True)]
where the time goes in v5:
time: 137 us
  blocking collectives  111 us (81%)
  starting transfers between devices  10.4 us (8%)
  waiting for transfers between devices  8.12 us (6%)
  Pallas kernels  5.4 us (4%)
    all_to_all x8, blocking collectives, exchange(): lax.all_to_all(message, axes, split_axis=0, concat_axis=0, tiled=True)  111 us
    all_to_all x1, starting transfers between devices, per_device(): lax.all_to_all(sensitivity.reshape(cases, depth, LANES), ('x', 'core'), s...  10.4 us
    all_to_all x1, waiting for transfers between devices, per_device(): lax.all_to_all(sensitivity.reshape(cases, depth, LANES), ('x', 'core'), s...  8.12 us
    pallas_call x3, Pallas kernels, per_device(): pl.pallas_call(functools.partial(middle_kernel, element_total), out_shape...  2.92 us
  transfers between devices with their start and end apart: 1, of which 1 were waited for; matrix products, arithmetic and copies ran while one was open for 0% of the time, Pallas kernels for 1%

profile of v5, /device:TPU:1, one launch (start us, length us, event | category | flops | bytes accessed | tf_op | source)
XLA Modules:
  0.0 136.7 jit_solution(5134628205625382026)
XLA Ops:
  0.6 0.0 copy-start
  0.6 0.0 copy-start.1
  0.7 0.0 copy-start.2
  0.7 0.0 copy-start.3
  0.7 0.0 copy-start.4
  0.7 0.0 copy-start.5
  0.7 10.4 %all-to-all-start = ((f32[8,128,128]{2,1,0:T(8,128)}), f32[8,128,128]{2,1,0:T(8,128)S(1)}, u32[]{:S(2)}, u32[]{:S(2)}) async-start(f32[8,128,128]{2,1,0:T(8,128)} %bitcast.52), calls=%async_computation | async-start | bytes 1048576 | tf_op jit(solution)/shard_map/all_to_all | solution.py:285
  11.1 0.0 copy-start.6
  11.1 0.0 copy-done
  11.1 0.0 copy-done.1
  11.1 0.0 copy-done.2
  11.1 0.0 copy-done.3
  11.1 0.0 copy-done.4
  11.2 0.0 copy-done.5
  11.2 0.6 copy-done.6
  11.8 0.0 copy-done.7
  11.8 0.7 shard_map.120
  12.5 8.1 %all-to-all-done = f32[8,128,128]{2,1,0:T(8,128)S(1)} async-done(((f32[8,128,128]{2,1,0:T(8,128)}), f32[8,128,128]{2,1,0:T(8,128)S(1)}, u32[]{:S(2)}, u32[]{:S(2)}) %all-to-all-start) | async-done | bytes 524320 | tf_op jit(solution)/shard_map/all_to_all | solution.py:285
  20.6 0.8 shard_map.121
  21.4 8.9 %all_to_all.73 = f32[16,1,128]{2,1,0:T(1,128)S(1)} all-to-all(f32[16,1,128]{2,1,0:T(1,128)S(1)} %bitcast.40), channel_id=1, replica_groups=mesh['x'=4,'core'=2,'y'=4,'z'=16] {'x','y'}, dimensions={0} | all-to-all | bytes 16384 | tf_op jit(solution)/shard_map/all_to_all | solution.py:290
  30.4 27.0 %all_to_all.74 = f32[32,1,128]{2,1,0:T(1,128)S(1)} all-to-all(f32[32,1,128]{2,1,0:T(1,128)S(1)} %broadcast_in_dim.8), channel_id=1, replica_groups=mesh['x'=4,'core'=2,'y'=4,'z'=16] {'core','z'}, dimensions={0} | all-to-all | bytes 32768 | tf_op jit(solution)/shard_map/all_to_all | solution.py:290
  57.3 1.0 shard_map.122
  58.3 9.1 %all_to_all.75 = f32[16,1,128]{2,1,0:T(1,128)S(1)} all-to-all(f32[16,1,128]{2,1,0:T(1,128)S(1)} %bitcast.43), channel_id=1, replica_groups=mesh['x'=4,'core'=2,'y'=4,'z'=16] {'x','y'}, dimensions={0} | all-to-all | bytes 16384 | tf_op jit(solution)/shard_map/all_to_all | solution.py:290
  67.5 16.5 %all_to_all.76 = f32[32,1,128]{2,1,0:T(1,128)S(1)} all-to-all(f32[32,1,128]{2,1,0:T(1,128)S(1)} %broadcast_in_dim.9), channel_id=1, replica_groups=mesh['x'=4,'core'=2,'y'=4,'z'=16] {'core','z'}, dimensions={0} | all-to-all | bytes 32768 | tf_op jit(solution)/shard_map/all_to_all | solution.py:290
  84.0 1.0 shard_map.123
  84.9 9.1 %all_to_all.77 = f32[16,1,128]{2,1,0:T(1,128)S(1)} all-to-all(f32[16,1,128]{2,1,0:T(1,128)S(1)} %bitcast.44), channel_id=1, replica_groups=mesh['x'=4,'core'=2,'y'=4,'z'=16] {'x','y'}, dimensions={0} | all-to-all | bytes 16384 | tf_op jit(solution)/shard_map/all_to_all | solution.py:290
  94.1 16.4 %all_to_all.78 = f32[32,1,128]{2,1,0:T(1,128)S(1)} all-to-all(f32[32,1,128]{2,1,0:T(1,128)S(1)} %broadcast_in_dim.10), channel_id=1, replica_groups=mesh['x'=4,'core'=2,'y'=4,'z'=16] {'core','z'}, dimensions={0} | all-to-all | bytes 32768 | tf_op jit(solution)/shard_map/all_to_all | solution.py:290
  110.6 1.0 shard_map.124
  111.5 15.0 %all_to_all.79 = f32[32,1,128]{2,1,0:T(1,128)S(1)} all-to-all(f32[32,1,128]{2,1,0:T(1,128)S(1)} %bitcast.42), channel_id=1, replica_groups=mesh['x'=4,'core'=2,'y'=4,'z'=16] {'core','z'}, dimensions={0} | all-to-all | bytes 32768 | tf_op jit(solution)/shard_map/all_to_all | solution.py:290
  126.5 0.1 reduce_sum.39
  126.6 9.1 %all_to_all.80 = f32[16,1,128]{2,1,0:T(1,128)S(1)} all-to-all(f32[16,1,128]{2,1,0:T(1,128)S(1)} %broadcast_in_dim.11), channel_id=1, replica_groups=mesh['x'=4,'core'=2,'y'=4,'z'=16] {'x','y'}, dimensions={0} | all-to-all | bytes 16384 | tf_op jit(solution)/shard_map/all_to_all | solution.py:290
  135.7 1.0 shard_map.125
  (8 shorter events, 0.2 us)
Async XLA Ops:
  0.6 10.5 %copy-start = (f32[1,1,16384]{2,1,0:T(1,128)S(1)}, f32[1,1,16384]{2,1,0:T(1,128)}, u32[]{:S(2)}) copy-start(f32[1,1,16384]{2,1,0:T(1,128)} %param.10) | copy-start | bytes 196612
  0.6 10.5 %copy-start.1 = (f32[1,1,16384]{2,1,0:T(1,128)S(1)}, f32[1,1,16384]{2,1,0:T(1,128)}, u32[]{:S(2)}) copy-start(f32[1,1,16384]{2,1,0:T(1,128)} %param.11) | copy-start | bytes 196612
  0.7 10.5 %copy-start.2 = (f32[1,1,16384]{2,1,0:T(1,128)S(1)}, f32[1,1,16384]{2,1,0:T(1,128)}, u32[]{:S(2)}) copy-start(f32[1,1,16384]{2,1,0:T(1,128)} %param.12) | copy-start | bytes 196612
  0.7 10.5 %copy-start.3 = (f32[1,1,16384]{2,1,0:T(1,128)S(1)}, f32[1,1,16384]{2,1,0:T(1,128)}, u32[]{:S(2)}) copy-start(f32[1,1,16384]{2,1,0:T(1,128)} %param.13) | copy-start | bytes 196612
  0.7 10.5 %copy-start.4 = (f32[1,1,16384]{2,1,0:T(1,128)S(1)}, f32[1,1,16384]{2,1,0:T(1,128)}, u32[]{:S(2)}) copy-start(f32[1,1,16384]{2,1,0:T(1,128)} %param.14) | copy-start | bytes 196612
  0.7 10.5 %copy-start.5 = (f32[1,1,16384]{2,1,0:T(1,128)S(1)}, f32[1,1,16384]{2,1,0:T(1,128)}, u32[]{:S(2)}) copy-start(f32[1,1,16384]{2,1,0:T(1,128)} %param.15) | copy-start | bytes 196612
  0.7 19.9 %all-to-all-start = ((f32[8,128,128]{2,1,0:T(8,128)}), f32[8,128,128]{2,1,0:T(8,128)S(1)}, u32[]{:S(2)}, u32[]{:S(2)}) async-start(f32[8,128,128]{2,1,0:T(8,128)} %bitcast.52), calls=%async_computation | async-start | bytes 1048576 | tf_op jit(solution)/shard_map/all_to_all | solution.py:285
  11.1 0.7 copy-start.6
  11.1 0.7 copy-start.7

commit v6 on v5

--- a/solution.py
+++ b/solution.py
@@ -21,7 +21,6 @@
 STATS = 64
 CHUNK = 128
 KUNROLL = 16
-ORDER = ("nf", "nf", "nf", "fn")
 
 
 def vmem():
@@ -261,8 +260,7 @@
 
 
 PARAMS = pltpu.CompilerParams(vmem_limit_bytes=16 * 1024 * 1024)
-NEAR = ("x", "y")
-FAR = ("core", "z")
+ORDER = ((("core", "x", "y"), ("z",)),) * (NEWTON - 1) + ((("core", "z"), ("x", "y")),)
 
 
 def scratch(blocks, depth):
@@ -275,11 +273,10 @@
 
 def per_device(sensitivity, x, x1, x2, gl, gu, w, case_values, duals_start):
     sizes = {name: lax.axis_size(name) for name in ("x", "core", "y", "z")}
-    near = sizes["x"] * sizes["y"]
-    far = sizes["core"] * sizes["z"]
+    devices = sizes["x"] * sizes["core"] * sizes["y"] * sizes["z"]
     cases = sizes["x"] * sizes["core"]
     depth = x.size // LANES
-    element_total = float(x.size * near * far)
+    element_total = float(x.size * devices)
     shape = x.shape
     x, x1, x2, gl, gu, w = (v.reshape(depth, LANES) for v in (x, x1, x2, gl, gu, w))
     g = lax.all_to_all(
@@ -289,12 +286,13 @@
     def exchange(message, axes):
         return lax.all_to_all(message, axes, split_axis=0, concat_axis=0, tiled=True)
 
-    stages = {"n": (NEAR, near), "f": (FAR, far)}
+    def count_of(axes):
+        return functools.reduce(lambda n, name: n * sizes[name], axes, 1)
 
     def gather(message, order):
-        (first, _), (second, count) = (stages[name] for name in order)
+        first, second = order
         part = jnp.sum(exchange(message, first), 0, keepdims=True)
-        return exchange(jnp.broadcast_to(part, (count, LANES)), second)
+        return exchange(jnp.broadcast_to(part, (count_of(second), LANES)), second)
 
     lower, upper, aux, volume, state = pl.pallas_call(
         prepare_kernel,
@@ -308,7 +306,7 @@
     )(duals_start.reshape(1, -1), case_values.reshape(1, -1), x, x1, x2, gl, gu, w)
     message = pl.pallas_call(
         first_kernel,
-        out_shape=f32(stages[ORDER[0][0]][1], LANES),
+        out_shape=f32(count_of(ORDER[0][0]), LANES),
         in_specs=[vmem()] * 4,
         out_specs=vmem(),
         scratch_shapes=scratch(1, depth)[:2],
@@ -317,7 +315,7 @@
     for step in range(1, NEWTON):
         state, message = pl.pallas_call(
             functools.partial(middle_kernel, element_total),
-            out_shape=(f32(STATE, LANES), f32(stages[ORDER[step][0]][1], LANES)),
+            out_shape=(f32(STATE, LANES), f32(count_of(ORDER[step][0]), LANES)),
             in_specs=[vmem()] * 4,
             out_specs=(vmem(),) * 2,
             scratch_shapes=scratch(1, depth),

time: 137 us -> 137 us (level)
  no operation moved by 1% of the time
where the time goes in v6:
time: 137 us
  blocking collectives  111 us (81%)
  starting transfers between devices  10.4 us (8%)
  waiting for transfers between devices  8.12 us (6%)
  Pallas kernels  5.39 us (4%)
    all_to_all x8, blocking collectives, exchange(): lax.all_to_all(message, axes, split_axis=0, concat_axis=0, tiled=True)  111 us
    all_to_all x1, starting transfers between devices, per_device(): lax.all_to_all(sensitivity.reshape(cases, depth, LANES), ('x', 'core'), s...  10.4 us
    all_to_all x1, waiting for transfers between devices, per_device(): lax.all_to_all(sensitivity.reshape(cases, depth, LANES), ('x', 'core'), s...  8.12 us
    pallas_call x3, Pallas kernels, per_device(): pl.pallas_call(functools.partial(middle_kernel, element_total), out_shape...  2.91 us
  transfers between devices with their start and end apart: 1, of which 1 were waited for; matrix products, arithmetic and copies ran while one was open for 0% of the time, Pallas kernels for 1%

profile of v6, /device:TPU:1, one launch (start us, length us, event | category | flops | bytes accessed | tf_op | source)
XLA Modules:
  0.0 136.8 jit_solution(11942790259771323148)
XLA Ops:
  0.6 0.0 copy-start
  0.6 0.0 copy-start.1
  0.7 0.0 copy-start.2
  0.7 0.0 copy-start.3
  0.7 0.0 copy-start.4
  0.7 0.0 copy-start.5
  0.7 10.4 %all-to-all-start = ((f32[8,128,128]{2,1,0:T(8,128)}), f32[8,128,128]{2,1,0:T(8,128)S(1)}, u32[]{:S(2)}, u32[]{:S(2)}) async-start(f32[8,128,128]{2,1,0:T(8,128)} %bitcast.52), calls=%async_computation | async-start | bytes 1048576 | tf_op jit(solution)/shard_map/all_to_all | solution.py:282
  11.1 0.0 copy-done
  11.1 0.0 copy-done.1
  11.1 0.0 copy-done.2
  11.1 0.0 copy-done.3
  11.2 0.6 copy-done.6
  11.8 0.0 copy-done.7
  11.8 0.7 shard_map.120
  12.5 8.1 %all-to-all-done = f32[8,128,128]{2,1,0:T(8,128)S(1)} async-done(((f32[8,128,128]{2,1,0:T(8,128)}), f32[8,128,128]{2,1,0:T(8,128)S(1)}, u32[]{:S(2)}, u32[]{:S(2)}) %all-to-all-start) | async-done | bytes 524320 | tf_op jit(solution)/shard_map/all_to_all | solution.py:282
  20.6 0.8 shard_map.121
  21.4 10.4 %all_to_all.73 = f32[32,1,128]{2,1,0:T(1,128)S(1)} all-to-all(f32[32,1,128]{2,1,0:T(1,128)S(1)} %bitcast.37), channel_id=1, replica_groups=mesh['x'=4,'core'=2,'y'=4,'z'=16] {'core','x','y'}, dimensions={0} | all-to-all | bytes 32768 | tf_op jit(solution)/shard_map/all_to_all | solution.py:287
  31.8 0.1 reduce_sum.36
  31.8 23.9 %all_to_all.74 = f32[16,1,128]{2,1,0:T(1,128)S(1)} all-to-all(f32[16,1,128]{2,1,0:T(1,128)S(1)} %broadcast_in_dim.8), channel_id=1, replica_groups=mesh['x'=4,'core'=2,'y'=4,'z'=16] {'z'}, dimensions={0} | all-to-all | bytes 16384 | tf_op jit(solution)/shard_map/all_to_all | solution.py:287
  55.7 1.0 shard_map.122
  56.7 12.0 %all_to_all.75 = f32[32,1,128]{2,1,0:T(1,128)S(1)} all-to-all(f32[32,1,128]{2,1,0:T(1,128)S(1)} %bitcast.42), channel_id=1, replica_groups=mesh['x'=4,'core'=2,'y'=4,'z'=16] {'core','x','y'}, dimensions={0} | all-to-all | bytes 32768 | tf_op jit(solution)/shard_map/all_to_all | solution.py:287
  68.7 0.1 reduce_sum.37
  68.8 13.8 %all_to_all.76 = f32[16,1,128]{2,1,0:T(1,128)S(1)} all-to-all(f32[16,1,128]{2,1,0:T(1,128)S(1)} %broadcast_in_dim.9), channel_id=1, replica_groups=mesh['x'=4,'core'=2,'y'=4,'z'=16] {'z'}, dimensions={0} | all-to-all | bytes 16384 | tf_op jit(solution)/shard_map/all_to_all | solution.py:287
  82.6 1.0 shard_map.123
  83.5 11.8 %all_to_all.77 = f32[32,1,128]{2,1,0:T(1,128)S(1)} all-to-all(f32[32,1,128]{2,1,0:T(1,128)S(1)} %bitcast.43), channel_id=1, replica_groups=mesh['x'=4,'core'=2,'y'=4,'z'=16] {'core','x','y'}, dimensions={0} | all-to-all | bytes 32768 | tf_op jit(solution)/shard_map/all_to_all | solution.py:287
  95.3 0.1 reduce_sum.38
  95.3 13.8 %all_to_all.78 = f32[16,1,128]{2,1,0:T(1,128)S(1)} all-to-all(f32[16,1,128]{2,1,0:T(1,128)S(1)} %broadcast_in_dim.10), channel_id=1, replica_groups=mesh['x'=4,'core'=2,'y'=4,'z'=16] {'z'}, dimensions={0} | all-to-all | bytes 16384 | tf_op jit(solution)/shard_map/all_to_all | solution.py:287
  109.2 1.0 shard_map.124
  110.1 16.5 %all_to_all.79 = f32[32,1,128]{2,1,0:T(1,128)S(1)} all-to-all(f32[32,1,128]{2,1,0:T(1,128)S(1)} %bitcast.44), channel_id=1, replica_groups=mesh['x'=4,'core'=2,'y'=4,'z'=16] {'core','z'}, dimensions={0} | all-to-all | bytes 32768 | tf_op jit(solution)/shard_map/all_to_all | solution.py:287
  126.6 0.1 reduce_sum.39
  126.7 9.1 %all_to_all.80 = f32[16,1,128]{2,1,0:T(1,128)S(1)} all-to-all(f32[16,1,128]{2,1,0:T(1,128)S(1)} %broadcast_in_dim.11), channel_id=1, replica_groups=mesh['x'=4,'core'=2,'y'=4,'z'=16] {'x','y'}, dimensions={0} | all-to-all | bytes 16384 | tf_op jit(solution)/shard_map/all_to_all | solution.py:287
  135.8 1.0 shard_map.125
  (8 shorter events, 0.0 us)
Async XLA Ops:
  0.6 10.5 %copy-start = (f32[1,1,16384]{2,1,0:T(1,128)S(1)}, f32[1,1,16384]{2,1,0:T(1,128)}, u32[]{:S(2)}) copy-start(f32[1,1,16384]{2,1,0:T(1,128)} %param.10) | copy-start | bytes 196612
  0.6 10.5 %copy-start.1 = (f32[1,1,16384]{2,1,0:T(1,128)S(1)}, f32[1,1,16384]{2,1,0:T(1,128)}, u32[]{:S(2)}) copy-start(f32[1,1,16384]{2,1,0:T(1,128)} %param.11) | copy-start | bytes 196612
  0.7 10.5 %copy-start.2 = (f32[1,1,16384]{2,1,0:T(1,128)S(1)}, f32[1,1,16384]{2,1,0:T(1,128)}, u32[]{:S(2)}) copy-start(f32[1,1,16384]{2,1,0:T(1,128)} %param.12) | copy-start | bytes 196612
  0.7 10.5 %copy-start.3 = (f32[1,1,16384]{2,1,0:T(1,128)S(1)}, f32[1,1,16384]{2,1,0:T(1,128)}, u32[]{:S(2)}) copy-start(f32[1,1,16384]{2,1,0:T(1,128)} %param.13) | copy-start | bytes 196612
  0.7 10.5 %copy-start.4 = (f32[1,1,16384]{2,1,0:T(1,128)S(1)}, f32[1,1,16384]{2,1,0:T(1,128)}, u32[]{:S(2)}) copy-start(f32[1,1,16384]{2,1,0:T(1,128)} %param.14) | copy-start | bytes 196612
  0.7 10.5 %copy-start.5 = (f32[1,1,16384]{2,1,0:T(1,128)S(1)}, f32[1,1,16384]{2,1,0:T(1,128)}, u32[]{:S(2)}) copy-start(f32[1,1,16384]{2,1,0:T(1,128)} %param.15) | copy-start | bytes 196612
  0.7 19.9 %all-to-all-start = ((f32[8,128,128]{2,1,0:T(8,128)}), f32[8,128,128]{2,1,0:T(8,128)S(1)}, u32[]{:S(2)}, u32[]{:S(2)}) async-start(f32[8,128,128]{2,1,0:T(8,128)} %bitcast.52), calls=%async_computation | async-start | bytes 1048576 | tf_op jit(solution)/shard_map/all_to_all | solution.py:282
  11.1 0.7 copy-start.6
  11.1 0.7 copy-start.7

commit v7 on v5

--- a/solution.py
+++ b/solution.py
@@ -261,7 +261,7 @@
 
 
 PARAMS = pltpu.CompilerParams(vmem_limit_bytes=16 * 1024 * 1024)
-NEAR = ("x", "y")
+NEAR = ("y", "x")
 FAR = ("core", "z")
 
 

time: 137 us -> 137 us (level)
  no operation moved by 1% of the time
where the time goes in v7:
time: 137 us
  blocking collectives  111 us (81%)
  starting transfers between devices  10.4 us (8%)
  waiting for transfers between devices  8.12 us (6%)
  Pallas kernels  5.4 us (4%)
    all_to_all x8, blocking collectives, exchange(): lax.all_to_all(message, axes, split_axis=0, concat_axis=0, tiled=True)  111 us
    all_to_all x1, starting transfers between devices, per_device(): lax.all_to_all(sensitivity.reshape(cases, depth, LANES), ('x', 'core'), s...  10.4 us
    all_to_all x1, waiting for transfers between devices, per_device(): lax.all_to_all(sensitivity.reshape(cases, depth, LANES), ('x', 'core'), s...  8.12 us
    pallas_call x3, Pallas kernels, per_device(): pl.pallas_call(functools.partial(middle_kernel, element_total), out_shape...  2.92 us
  transfers between devices with their start and end apart: 1, of which 1 were waited for; matrix products, arithmetic and copies ran while one was open for 0% of the time, Pallas kernels for 1%

profile of v7, /device:TPU:1, one launch (start us, length us, event | category | flops | bytes accessed | tf_op | source)
XLA Modules:
  0.0 136.7 jit_solution(14223773929169549899)
XLA Ops:
  0.6 0.0 copy-start
  0.6 0.0 copy-start.1
  0.7 0.0 copy-start.2
  0.7 0.0 copy-start.3
  0.7 0.0 copy-start.4
  0.7 0.0 copy-start.5
  0.7 10.4 %all-to-all-start = ((f32[8,128,128]{2,1,0:T(8,128)}), f32[8,128,128]{2,1,0:T(8,128)S(1)}, u32[]{:S(2)}, u32[]{:S(2)}) async-start(f32[8,128,128]{2,1,0:T(8,128)} %bitcast.52), calls=%async_computation | async-start | bytes 1048576 | tf_op jit(solution)/shard_map/all_to_all | solution.py:285
  11.1 0.0 copy-start.6
  11.1 0.0 copy-done
  11.1 0.0 copy-done.1
  11.1 0.0 copy-done.2
  11.1 0.0 copy-done.3
  11.1 0.0 copy-done.4
  11.2 0.0 copy-done.5
  11.2 0.6 copy-done.6
  11.8 0.0 copy-done.7
  11.8 0.7 shard_map.120
  12.5 8.1 %all-to-all-done = f32[8,128,128]{2,1,0:T(8,128)S(1)} async-done(((f32[8,128,128]{2,1,0:T(8,128)}), f32[8,128,128]{2,1,0:T(8,128)S(1)}, u32[]{:S(2)}, u32[]{:S(2)}) %all-to-all-start) | async-done | bytes 524320 | tf_op jit(solution)/shard_map/all_to_all | solution.py:285
  20.6 0.8 shard_map.121
  21.4 8.9 %all_to_all.73 = f32[16,1,128]{2,1,0:T(1,128)S(1)} all-to-all(f32[16,1,128]{2,1,0:T(1,128)S(1)} %bitcast.40), channel_id=1, replica_groups=mesh['x'=4,'core'=2,'y'=4,'z'=16] {'y','x'}, dimensions={0} | all-to-all | bytes 16384 | tf_op jit(solution)/shard_map/all_to_all | solution.py:290
  30.4 27.0 %all_to_all.74 = f32[32,1,128]{2,1,0:T(1,128)S(1)} all-to-all(f32[32,1,128]{2,1,0:T(1,128)S(1)} %broadcast_in_dim.8), channel_id=1, replica_groups=mesh['x'=4,'core'=2,'y'=4,'z'=16] {'core','z'}, dimensions={0} | all-to-all | bytes 32768 | tf_op jit(solution)/shard_map/all_to_all | solution.py:290
  57.3 1.0 shard_map.122
  58.3 9.1 %all_to_all.75 = f32[16,1,128]{2,1,0:T(1,128)S(1)} all-to-all(f32[16,1,128]{2,1,0:T(1,128)S(1)} %bitcast.43), channel_id=1, replica_groups=mesh['x'=4,'core'=2,'y'=4,'z'=16] {'y','x'}, dimensions={0} | all-to-all | bytes 16384 | tf_op jit(solution)/shard_map/all_to_all | solution.py:290
  67.5 16.5 %all_to_all.76 = f32[32,1,128]{2,1,0:T(1,128)S(1)} all-to-all(f32[32,1,128]{2,1,0:T(1,128)S(1)} %broadcast_in_dim.9), channel_id=1, replica_groups=mesh['x'=4,'core'=2,'y'=4,'z'=16] {'core','z'}, dimensions={0} | all-to-all | bytes 32768 | tf_op jit(solution)/shard_map/all_to_all | solution.py:290
  84.0 1.0 shard_map.123
  84.9 9.1 %all_to_all.77 = f32[16,1,128]{2,1,0:T(1,128)S(1)} all-to-all(f32[16,1,128]{2,1,0:T(1,128)S(1)} %bitcast.44), channel_id=1, replica_groups=mesh['x'=4,'core'=2,'y'=4,'z'=16] {'y','x'}, dimensions={0} | all-to-all | bytes 16384 | tf_op jit(solution)/shard_map/all_to_all | solution.py:290
  94.1 16.4 %all_to_all.78 = f32[32,1,128]{2,1,0:T(1,128)S(1)} all-to-all(f32[32,1,128]{2,1,0:T(1,128)S(1)} %broadcast_in_dim.10), channel_id=1, replica_groups=mesh['x'=4,'core'=2,'y'=4,'z'=16] {'core','z'}, dimensions={0} | all-to-all | bytes 32768 | tf_op jit(solution)/shard_map/all_to_all | solution.py:290
  110.5 1.0 shard_map.124
  111.5 15.0 %all_to_all.79 = f32[32,1,128]{2,1,0:T(1,128)S(1)} all-to-all(f32[32,1,128]{2,1,0:T(1,128)S(1)} %bitcast.42), channel_id=1, replica_groups=mesh['x'=4,'core'=2,'y'=4,'z'=16] {'core','z'}, dimensions={0} | all-to-all | bytes 32768 | tf_op jit(solution)/shard_map/all_to_all | solution.py:290
  126.5 0.1 reduce_sum.39
  126.6 9.1 %all_to_all.80 = f32[16,1,128]{2,1,0:T(1,128)S(1)} all-to-all(f32[16,1,128]{2,1,0:T(1,128)S(1)} %broadcast_in_dim.11), channel_id=1, replica_groups=mesh['x'=4,'core'=2,'y'=4,'z'=16] {'y','x'}, dimensions={0} | all-to-all | bytes 16384 | tf_op jit(solution)/shard_map/all_to_all | solution.py:290
  135.7 1.0 shard_map.125
  (8 shorter events, 0.2 us)
Async XLA Ops:
  0.6 10.5 %copy-start = (f32[1,1,16384]{2,1,0:T(1,128)S(1)}, f32[1,1,16384]{2,1,0:T(1,128)}, u32[]{:S(2)}) copy-start(f32[1,1,16384]{2,1,0:T(1,128)} %param.10) | copy-start | bytes 196612
  0.6 10.5 %copy-start.1 = (f32[1,1,16384]{2,1,0:T(1,128)S(1)}, f32[1,1,16384]{2,1,0:T(1,128)}, u32[]{:S(2)}) copy-start(f32[1,1,16384]{2,1,0:T(1,128)} %param.11) | copy-start | bytes 196612
  0.7 10.5 %copy-start.2 = (f32[1,1,16384]{2,1,0:T(1,128)S(1)}, f32[1,1,16384]{2,1,0:T(1,128)}, u32[]{:S(2)}) copy-start(f32[1,1,16384]{2,1,0:T(1,128)} %param.12) | copy-start | bytes 196612
  0.7 10.5 %copy-start.3 = (f32[1,1,16384]{2,1,0:T(1,128)S(1)}, f32[1,1,16384]{2,1,0:T(1,128)}, u32[]{:S(2)}) copy-start(f32[1,1,16384]{2,1,0:T(1,128)} %param.13) | copy-start | bytes 196612
  0.7 10.5 %copy-start.4 = (f32[1,1,16384]{2,1,0:T(1,128)S(1)}, f32[1,1,16384]{2,1,0:T(1,128)}, u32[]{:S(2)}) copy-start(f32[1,1,16384]{2,1,0:T(1,128)} %param.14) | copy-start | bytes 196612
  0.7 10.5 %copy-start.5 = (f32[1,1,16384]{2,1,0:T(1,128)S(1)}, f32[1,1,16384]{2,1,0:T(1,128)}, u32[]{:S(2)}) copy-start(f32[1,1,16384]{2,1,0:T(1,128)} %param.15) | copy-start | bytes 196612
  0.7 19.9 %all-to-all-start = ((f32[8,128,128]{2,1,0:T(8,128)}), f32[8,128,128]{2,1,0:T(8,128)S(1)}, u32[]{:S(2)}, u32[]{:S(2)}) async-start(f32[8,128,128]{2,1,0:T(8,128)} %bitcast.52), calls=%async_computation | async-start | bytes 1048576 | tf_op jit(solution)/shard_map/all_to_all | solution.py:285
  11.1 0.7 copy-start.6
  11.1 0.7 copy-start.7

commit v8 on v7

--- a/solution.py
+++ b/solution.py
@@ -21,7 +21,7 @@
 STATS = 64
 CHUNK = 128
 KUNROLL = 16
-ORDER = ("nf", "nf", "nf", "fn")
+ORDER = ("nf", "nf", "nf", "pz")
 
 
 def vmem():
@@ -289,7 +289,7 @@
     def exchange(message, axes):
         return lax.all_to_all(message, axes, split_axis=0, concat_axis=0, tiled=True)
 
-    stages = {"n": (NEAR, near), "f": (FAR, far)}
+    stages = {"n": (NEAR, near), "f": (FAR, far), "p": (("core",) + NEAR, sizes["core"] * near), "z": (("z",), sizes["z"])}
 
     def gather(message, order):
         (first, _), (second, count) = (stages[name] for name in order)

time: 137 us -> 137 us (level)
  no operation moved by 1% of the time
where the time goes in v8:
time: 137 us
  blocking collectives  111 us (81%)
  starting transfers between devices  10.4 us (8%)
  waiting for transfers between devices  8.12 us (6%)
  Pallas kernels  5.4 us (4%)
    all_to_all x8, blocking collectives, exchange(): lax.all_to_all(message, axes, split_axis=0, concat_axis=0, tiled=True)  111 us
    all_to_all x1, starting transfers between devices, per_device(): lax.all_to_all(sensitivity.reshape(cases, depth, LANES), ('x', 'core'), s...  10.4 us
    all_to_all x1, waiting for transfers between devices, per_device(): lax.all_to_all(sensitivity.reshape(cases, depth, LANES), ('x', 'core'), s...  8.12 us
    pallas_call x3, Pallas kernels, per_device(): pl.pallas_call(functools.partial(middle_kernel, element_total), out_shape...  2.92 us
  transfers between devices with their start and end apart: 1, of which 1 were waited for; matrix products, arithmetic and copies ran while one was open for 0% of the time, Pallas kernels for 1%

profile of v8, /device:TPU:1, one launch (start us, length us, event | category | flops | bytes accessed | tf_op | source)
XLA Modules:
  0.0 136.7 jit_solution(3776159236171135566)
XLA Ops:
  0.6 0.0 copy-start
  0.6 0.0 copy-start.1
  0.7 0.0 copy-start.2
  0.7 0.0 copy-start.3
  0.7 0.0 copy-start.4
  0.7 0.0 copy-start.5
  0.7 10.4 %all-to-all-start = ((f32[8,128,128]{2,1,0:T(8,128)}), f32[8,128,128]{2,1,0:T(8,128)S(1)}, u32[]{:S(2)}, u32[]{:S(2)}) async-start(f32[8,128,128]{2,1,0:T(8,128)} %bitcast.52), calls=%async_computation | async-start | bytes 1048576 | tf_op jit(solution)/shard_map/all_to_all | solution.py:285
  11.1 0.0 copy-start.6
  11.1 0.0 copy-done
  11.1 0.0 copy-done.1
  11.1 0.0 copy-done.2
  11.1 0.0 copy-done.3
  11.1 0.0 copy-done.4
  11.2 0.0 copy-done.5
  11.2 0.6 copy-done.6
  11.8 0.0 copy-done.7
  11.8 0.7 shard_map.120
  12.5 8.1 %all-to-all-done = f32[8,128,128]{2,1,0:T(8,128)S(1)} async-done(((f32[8,128,128]{2,1,0:T(8,128)}), f32[8,128,128]{2,1,0:T(8,128)S(1)}, u32[]{:S(2)}, u32[]{:S(2)}) %all-to-all-start) | async-done | bytes 524320 | tf_op jit(solution)/shard_map/all_to_all | solution.py:285
  20.6 0.8 shard_map.121
  21.4 8.9 %all_to_all.73 = f32[16,1,128]{2,1,0:T(1,128)S(1)} all-to-all(f32[16,1,128]{2,1,0:T(1,128)S(1)} %bitcast.40), channel_id=1, replica_groups=mesh['x'=4,'core'=2,'y'=4,'z'=16] {'y','x'}, dimensions={0} | all-to-all | bytes 16384 | tf_op jit(solution)/shard_map/all_to_all | solution.py:290
  30.4 27.0 %all_to_all.74 = f32[32,1,128]{2,1,0:T(1,128)S(1)} all-to-all(f32[32,1,128]{2,1,0:T(1,128)S(1)} %broadcast_in_dim.8), channel_id=1, replica_groups=mesh['x'=4,'core'=2,'y'=4,'z'=16] {'core','z'}, dimensions={0} | all-to-all | bytes 32768 | tf_op jit(solution)/shard_map/all_to_all | solution.py:290
  57.3 1.0 shard_map.122
  58.3 9.1 %all_to_all.75 = f32[16,1,128]{2,1,0:T(1,128)S(1)} all-to-all(f32[16,1,128]{2,1,0:T(1,128)S(1)} %bitcast.43), channel_id=1, replica_groups=mesh['x'=4,'core'=2,'y'=4,'z'=16] {'y','x'}, dimensions={0} | all-to-all | bytes 16384 | tf_op jit(solution)/shard_map/all_to_all | solution.py:290
  67.5 16.5 %all_to_all.76 = f32[32,1,128]{2,1,0:T(1,128)S(1)} all-to-all(f32[32,1,128]{2,1,0:T(1,128)S(1)} %broadcast_in_dim.9), channel_id=1, replica_groups=mesh['x'=4,'core'=2,'y'=4,'z'=16] {'core','z'}, dimensions={0} | all-to-all | bytes 32768 | tf_op jit(solution)/shard_map/all_to_all | solution.py:290
  84.0 1.0 shard_map.123
  84.9 9.1 %all_to_all.77 = f32[16,1,128]{2,1,0:T(1,128)S(1)} all-to-all(f32[16,1,128]{2,1,0:T(1,128)S(1)} %bitcast.44), channel_id=1, replica_groups=mesh['x'=4,'core'=2,'y'=4,'z'=16] {'y','x'}, dimensions={0} | all-to-all | bytes 16384 | tf_op jit(solution)/shard_map/all_to_all | solution.py:290
  94.1 16.4 %all_to_all.78 = f32[32,1,128]{2,1,0:T(1,128)S(1)} all-to-all(f32[32,1,128]{2,1,0:T(1,128)S(1)} %broadcast_in_dim.10), channel_id=1, replica_groups=mesh['x'=4,'core'=2,'y'=4,'z'=16] {'core','z'}, dimensions={0} | all-to-all | bytes 32768 | tf_op jit(solution)/shard_map/all_to_all | solution.py:290
  110.5 1.0 shard_map.124
  111.5 10.3 %all_to_all.79 = f32[32,1,128]{2,1,0:T(1,128)S(1)} all-to-all(f32[32,1,128]{2,1,0:T(1,128)S(1)} %bitcast.42), channel_id=1, replica_groups=mesh['x'=4,'core'=2,'y'=4,'z'=16] {'core','y','x'}, dimensions={0} | all-to-all | bytes 32768 | tf_op jit(solution)/shard_map/all_to_all | solution.py:290
  121.8 0.1 reduce_sum.39
  121.8 13.8 %all_to_all.80 = f32[16,1,128]{2,1,0:T(1,128)S(1)} all-to-all(f32[16,1,128]{2,1,0:T(1,128)S(1)} %broadcast_in_dim.11), channel_id=1, replica_groups=mesh['x'=4,'core'=2,'y'=4,'z'=16] {'z'}, dimensions={0} | all-to-all | bytes 16384 | tf_op jit(solution)/shard_map/all_to_all | solution.py:290
  135.6 1.0 shard_map.125
  (8 shorter events, 0.2 us)
Async XLA Ops:
  0.6 10.5 %copy-start = (f32[1,1,16384]{2,1,0:T(1,128)S(1)}, f32[1,1,16384]{2,1,0:T(1,128)}, u32[]{:S(2)}) copy-start(f32[1,1,16384]{2,1,0:T(1,128)} %param.10) | copy-start | bytes 196612
  0.6 10.5 %copy-start.1 = (f32[1,1,16384]{2,1,0:T(1,128)S(1)}, f32[1,1,16384]{2,1,0:T(1,128)}, u32[]{:S(2)}) copy-start(f32[1,1,16384]{2,1,0:T(1,128)} %param.11) | copy-start | bytes 196612
  0.7 10.5 %copy-start.2 = (f32[1,1,16384]{2,1,0:T(1,128)S(1)}, f32[1,1,16384]{2,1,0:T(1,128)}, u32[]{:S(2)}) copy-start(f32[1,1,16384]{2,1,0:T(1,128)} %param.12) | copy-start | bytes 196612
  0.7 10.5 %copy-start.3 = (f32[1,1,16384]{2,1,0:T(1,128)S(1)}, f32[1,1,16384]{2,1,0:T(1,128)}, u32[]{:S(2)}) copy-start(f32[1,1,16384]{2,1,0:T(1,128)} %param.13) | copy-start | bytes 196612
  0.7 10.5 %copy-start.4 = (f32[1,1,16384]{2,1,0:T(1,128)S(1)}, f32[1,1,16384]{2,1,0:T(1,128)}, u32[]{:S(2)}) copy-start(f32[1,1,16384]{2,1,0:T(1,128)} %param.14) | copy-start | bytes 196612
  0.7 10.5 %copy-start.5 = (f32[1,1,16384]{2,1,0:T(1,128)S(1)}, f32[1,1,16384]{2,1,0:T(1,128)}, u32[]{:S(2)}) copy-start(f32[1,1,16384]{2,1,0:T(1,128)} %param.15) | copy-start | bytes 196612
  0.7 19.9 %all-to-all-start = ((f32[8,128,128]{2,1,0:T(8,128)}), f32[8,128,128]{2,1,0:T(8,128)S(1)}, u32[]{:S(2)}, u32[]{:S(2)}) async-start(f32[8,128,128]{2,1,0:T(8,128)} %bitcast.52), calls=%async_computation | async-start | bytes 1048576 | tf_op jit(solution)/shard_map/all_to_all | solution.py:285
  11.1 0.7 copy-start.6
  11.1 0.7 copy-start.7
